TPU v7x, 256 devices: a whole 4x4x8 slice. The times are simulated.
256 devices in a mesh: slab: 16 (over x_lo, y, core), blk: 16 (over z, x_hi).
Axes of the slice: x: 4 (x_hi: 2, x_lo: 2; x = x_hi * 2 + x_lo), y: 4, z: 8, core: 2. Of those that a mesh axis runs over, the one named last changes fastest.
Arguments:
- amplitude: float32 [1024, 2048], P('blk'), may hold values from -6 to 6
- integrals: float32 [2048, 16, 16, 800], P(None, 'slab', 'blk'), may hold values from -0.375 to 0.375
- row_irrep: int32 [128], replicated, may hold values from 0 to 7
- cd_irrep: int32 [16], replicated, may hold values from 0 to 7
- a_irrep: int32 [16, 16], replicated, may hold values from 0 to 7
- owner: int32 [128, 1], replicated, may hold values from 0 to 15; in each aligned block of 128 rows (0 to 127, 128 to 255, ...) at most 16 rows name the same one
Outputs:
- owned: float32 [2048, 16, 16, 800], P('slab', None, 'blk')
Inputs may be any that keep to these rules, and one draw needn't show every extreme that they name: `owner`: no slab index owns more than 16 tiles, and some slab index owns exactly 16.
All inputs are finite; a program needn't handle non-finite values.
Results may differ from a plain program's by a relative error of at most 0.000071.
Values sent between devices are 32-bit elements; how exact they have to be, the bound alone decides.
A program may use at most 128 MiB of HBM per device.

v0:
```python
import jax
import jax.numpy as jnp
from jax import lax
from jax.sharding import PartitionSpec as P

IRREPS = 8
CD_TILE = 128
ROW_TILE = 8


def slot_sources(owner, n_slab, capacity):
    owners = owner[:, 0]
    ntiles = owners.shape[0]
    onehot = (owners[:, None] == jnp.arange(n_slab, dtype=jnp.int32)[None, :]).astype(jnp.int32)
    before = jnp.cumsum(onehot, axis=0) - onehot
    rank = jnp.sum(before * onehot, axis=1)
    target = owners * capacity + rank
    slots = jnp.arange(n_slab * capacity, dtype=jnp.int32)
    match = target[None, :] == slots[:, None]
    source = jnp.sum(jnp.where(match, jnp.arange(ntiles, dtype=jnp.int32)[None, :], 0), axis=1)
    filled = jnp.any(match, axis=1)
    return (match, source, filled)


def shards(amplitude, integrals, row_irrep, cd_irrep, a_irrep, owner):
    n_slab = lax.axis_size("slab")
    n_blk = lax.axis_size("blk")
    slab_index = lax.axis_index("slab")
    blk_index = lax.axis_index("blk")
    cdpairs = amplitude.shape[1]
    a_count = integrals.shape[2]
    nvirt = integrals.shape[3]
    vblock = nvirt // IRREPS
    tiles = amplitude.shape[0] * n_blk // ROW_TILE
    capacity = 2 * tiles // n_slab
    column_labels = jnp.take(cd_irrep, jnp.arange(cdpairs, dtype=jnp.int32) // CD_TILE)
    vir_labels = jnp.arange(nvirt, dtype=jnp.int32) // vblock
    irrep_ids = jnp.arange(IRREPS, dtype=jnp.int32)
    a_block = lax.dynamic_slice_in_dim(a_irrep, blk_index * a_count, a_count, 1)
    own_a = lax.dynamic_index_in_dim(a_block, slab_index, 0, keepdims=False)
    own_pairs = jnp.bitwise_xor(own_a[:, None], vir_labels[None, :]).reshape(-1)
    match, source, filled = slot_sources(owner, n_slab, capacity)
    flat = integrals.reshape(cdpairs, a_count * nvirt)
    piece = lax.all_gather(amplitude, "blk", axis=0, tiled=True)
    count = piece.shape[0]
    rows = jnp.arange(count, dtype=jnp.int32) // ROW_TILE
    labels = jnp.take(row_irrep, rows)
    coupled = jnp.where(labels[:, None] == column_labels[None, :], piece, 0.0)
    product = jnp.dot(
        coupled, flat, precision=lax.Precision.HIGHEST, preferred_element_type=jnp.float32
    )
    ladder = jnp.where(labels[:, None] == own_pairs[None, :], product, 0.0)
    split_blocks = ladder.reshape(tiles, ROW_TILE, a_count, IRREPS, vblock)
    wanted = jnp.bitwise_xor(row_irrep[:, None], own_a[None, :])
    select = wanted[:, None, :, None, None] == irrep_ids[None, None, None, :, None]
    send_tiles = jnp.sum(jnp.where(select, split_blocks, 0.0), axis=3).reshape(tiles, -1)
    packed = jnp.dot(
        match.astype(jnp.float32),
        send_tiles,
        precision=lax.Precision.HIGHEST,
        preferred_element_type=jnp.float32,
    )
    packed = packed.reshape(n_slab * capacity * ROW_TILE, 1, a_count, vblock)
    arrived = lax.all_to_all(packed, "slab", split_axis=0, concat_axis=1, tiled=True)
    mine = lax.dynamic_slice_in_dim(source, slab_index * capacity, capacity, 0)
    slot_labels = jnp.repeat(jnp.take(row_irrep, mine), ROW_TILE)
    target_labels = jnp.bitwise_xor(slot_labels[:, None, None], a_block[None, :, :])
    place = target_labels[:, :, :, None, None] == irrep_ids[None, None, None, :, None]
    expanded = jnp.where(place, arrived[:, :, :, None, :], 0.0)
    return expanded.reshape(capacity * ROW_TILE, n_slab, a_count, nvirt)


def solution(mesh):
    return jax.shard_map(
        shards,
        mesh=mesh,
        in_specs=(P("blk", None), P(None, "slab", "blk", None), P(), P(), P(), P()),
        out_specs=P("slab", None, "blk", None),
        check_vma=False,
    )
```

profile of v0, /device:TPU:1, one launch (start us, length us, event | category | flops | bytes accessed | tf_op | source)
XLA Modules:
  0.0 230.6 jit_solution(7752692102180760596)
XLA Ops:
  6.5 0.7 all-gather.2.cloned.1.call-update
  7.3 0.7 fusion.13
  8.0 0.2 reduce_window_sum.11
  8.2 5.9 %gather_fusion.1 = s32[1024]{0:T(1024)S(1)} fusion(s32[128]{0:T(128)} %param.8, s32[1024]{0:T(1024)S(1)} %broadcast_clamp_fusion), kind=kCustom, calls=%fused_computation.1 | custom fusion | bytes 12288 | tf_op jit(solution)/shard_map/jit(_take)/gather | solution.py:47
  14.1 1.3 dynamic_slice.12
  15.7 0.8 select_reduce_fusion.2
  16.5 0.7 multiply_add_fusion
  17.2 0.1 select_reduce_fusion.1
  17.3 0.1 compare_select_fusion.11
  17.4 0.6 fusion.20
  18.0 2.0 fusion.32
  19.9 1.2 broadcast_xor_fusion.1
  21.2 4.4 %compare_select_fusion.2 = s32[2048,1]{0,1:T(1,128)S(1)} fusion(s32[]{:T(128)} %bitcast.12, s32[]{:T(128)} %bitcast.13, s32[]{:T(128)} %bitcast.14, s32[]{:T(128)} %bitcast.15, s32[]{:T(128)} %bitcast.16, s32[]{:T(128)} %bitcast.18, s32[]{:T(128)} %bitcast.17), kind=kLoop, calls=%fused_computation.31 | loop fusion | flops 47104 | bytes 8220 | tf_op jit(solution)/shard_map/jit(_take)/gather | solution.py:36
  25.6 0.1 iota_compare_fusion.2
  25.7 5.6 %select_select_fusion = s32[2048]{0:T(1024)S(1)} fusion(pred[2048]{0:T(1024)(128)(4,1)S(1)} %compare_reduce_fusion, pred[2048]{0:T(1024)(128)(4,1)S(1)} %compare_reduce_fusion.1, pred[2048]{0:T(1024)(128)(4,1)S(1)} %compare_reduce_fusion.2, pred[2048]{0:T(1024)(128)(4,1)S(1)} %compare_reduce_fusion.3, pred[2048]{0:T(1024)(128)(4,1)S(1)} %compare_reduce_fusion.4, ...), kind=kLoop, calls=%fused_computation.53 | loop fusion | flops 49152 | bytes 34852 | tf_op jit(solution)/shard_map/jit(_take)/select_n | solution.py:36
  31.3 117.8 %all-gather.2.cloned.1.call-done = f32[1024,2048]{1,0:T(8,128)} async-done(((f32[64,2048]{1,0:T(8,128)}), f32[1024,2048]{1,0:T(8,128)}) %all-gather.2.cloned.1.call-update) | async-done | bytes 8388624 | tf_op jit(solution)/shard_map/all_gather | solution.py:44
  149.0 30.6 %compare_select_fusion = f32[1024,800]{0,1:T(8,128)S(1)} fusion(f32[2048,1,1,800]{0,3,2,1:T(8,128)} %param.7, f32[1024,2048]{1,0:T(8,128)} %all-gather.2.cloned.1.call-done, s32[2048]{0:T(1024)S(1)} %select_select_fusion, s32[1024]{0:T(1024)S(1)} %fusion.28, s32[800]{0:T(1024)S(1)} %fusion.20), kind=kOutput, calls=%fused_computation.11 | convolution fusion | flops 20138491904 | bytes 18234496 | tf_op jit(solution)/shard_map/dot_general | solution.py:49
  179.7 3.3 %copy.17 = f32[1024,800]{1,0:T(8,128)} copy(f32[1024,800]{0,1:T(8,128)S(1)} %compare_select_fusion) | data formatting | bytes 6553600 | tf_op jit(solution)/shard_map/jit(_where)/select_n | solution.py:52
  183.0 5.6 %reshape.291 = f32[128,8,1,8,100]{4,3,1,0,2:T(8,128)} reshape(f32[1024,800]{1,0:T(8,128)} %copy.17) | data formatting | bytes 6553600 | tf_op jit(solution)/shard_map/reshape | solution.py:53
  188.6 3.7 %select_reduce_fusion = f32[128,8,100]{2,1,0:T(8,128)S(1)} fusion(f32[128,8,1,8,100]{4,3,1,0,2:T(8,128)} %reshape.291, pred[128,8]{1,0:T(8,128)(4,1)S(1)} %iota_compare_fusion.2), kind=kLoop, calls=%fused_computation.6 | loop fusion | flops 1536000 | bytes 3687424 | tf_op jit(solution)/shard_map/reduce_sum | solution.py:56
  192.3 0.2 reshape.379
  192.5 0.5 fusion.11
  193.0 1.5 reshape.293
  194.5 5.4 %all-to-all-start = ((f32[2048,1,1,100]{3,2,1,0:T(1,128)}), f32[2048,1,1,100]{3,2,1,0:T(1,128)S(1)}, u32[]{:S(2)}, u32[]{:S(2)}) async-start(f32[2048,1,1,100]{3,2,1,0:T(1,128)} %bitcast.21), calls=%async_computation | async-start | bytes 2097152 | tf_op jit(solution)/shard_map/all_to_all | solution.py:64
  199.9 0.7 gather_fusion
  200.6 0.1 and_select_fusion.2
  200.7 0.1 xor.47
  200.9 0.2 dynamic-slice_reduce_fusion
  201.1 14.6 %all-to-all-done = f32[2048,1,1,100]{3,2,1,0:T(1,128)S(1)} async-done(((f32[2048,1,1,100]{3,2,1,0:T(1,128)}), f32[2048,1,1,100]{3,2,1,0:T(1,128)S(1)}, u32[]{:S(2)}, u32[]{:S(2)}) %all-to-all-start) | async-done | bytes 819232 | tf_op jit(solution)/shard_map/all_to_all | solution.py:64
  215.7 2.7 %copy.21 = f32[2048,1,1,100]{0,2,3,1:T(1,128)S(1)} copy(f32[2048,1,1,100]{3,2,1,0:T(1,128)S(1)} %all-to-all-done) | data formatting | bytes 1638400 | tf_op jit(solution)/shard_map/all_to_all | solution.py:64
  218.4 0.6 broadcast_select_fusion
  219.0 4.8 %copy.22 = f32[128,16,1,800]{0,3,2,1:T(8,128)} copy(f32[128,16,1,800]{0,1,3,2:T(8,128)S(1)} %bitcast.34) | data formatting | bytes 13107200 | tf_op jit(solution)/shard_map/jit(_where)/select_n | solution.py:69
  (21 shorter events, 0.6 us)
Async XLA Ops:
  6.5 142.5 %all-gather.2.cloned.1.call-start = ((), (), s32[]{:S(2)}) async-start(), calls=%async_computation.1 | async-start | bytes 8912896 | tf_op jit(solution)/shard_map/all_gather | solution.py:44
  188.6 11.4 %copy-start = (s32[128]{0:T(128)S(1)}, s32[128]{0:T(128)}, u32[]{:S(2)}) copy-start(s32[128]{0:T(128)} %param.8) | copy-start | bytes 1540
  188.6 12.3 %copy-start.1 = (s32[16,16]{1,0:T(8,128)S(1)}, s32[16,16]{1,0:T(8,128)}, u32[]{:S(2)}) copy-start(s32[16,16]{1,0:T(8,128)} %param.10) | copy-start | bytes 3076
  194.5 21.2 %all-to-all-start = ((f32[2048,1,1,100]{3,2,1,0:T(1,128)}), f32[2048,1,1,100]{3,2,1,0:T(1,128)S(1)}, u32[]{:S(2)}, u32[]{:S(2)}) async-start(f32[2048,1,1,100]{3,2,1,0:T(1,128)} %bitcast.21), calls=%async_computation | async-start | bytes 2097152 | tf_op jit(solution)/shard_map/all_to_all | solution.py:64
Sparse Core Ops, SparseCore 0:
  9.9 139.0 all-gather.1
where the time goes:
time: 231 us
  waiting for transfers between devices  133 us (58%)
  matrix products  31.2 us (14%)
  local copies, waits for them, and re-layouts  28.2 us (12%)
  other arithmetic  19.3 us (8%)
  between operations  13.6 us (6%)
  starting transfers between devices  5.39 us (2%)
    all_gather x1, waiting for transfers between devices, shards(): piece = lax.all_gather(amplitude, 'blk', axis=0, tiled=True)  118 us
    dot_general x1, matrix products, shards(): jnp.dot(coupled, flat, precision=lax.Precision.HIGHEST, preferred_element...  30.6 us
    all_to_all x1, waiting for transfers between devices, shards(): lax.all_to_all(packed, 'slab', split_axis=0, concat_axis=1, tiled=True)  14.6 us
    gather x1, local copies, waits for them, and re-layouts, shards(): labels = jnp.take(row_irrep, rows)  5.85 us
    reshape x1, local copies, waits for them, and re-layouts, shards(): split_blocks = ladder.reshape(tiles, ROW_TILE, a_count, IRREPS, vblock)  5.58 us
    select_n x1, other arithmetic, shards(): jnp.take(cd_irrep, jnp.arange(cdpairs, dtype=jnp.int32) // CD_TILE)  5.57 us
    all_to_all x1, starting transfers between devices, shards(): lax.all_to_all(packed, 'slab', split_axis=0, concat_axis=1, tiled=True)  5.39 us
    gather x10, other arithmetic, shards(): jnp.take(cd_irrep, jnp.arange(cdpairs, dtype=jnp.int32) // CD_TILE)  4.79 us
  transfers between devices with their start and end apart: 2, of which 2 were waited for; matrix products, arithmetic and copies ran while one was open for 11% of the time, Pallas kernels for 0%

commit v1 on v0

v1 whole, which is shorter than its diff:
```python
import functools

import jax
import jax.numpy as jnp
from jax import lax
from jax.experimental import pallas as pl
from jax.experimental.pallas import tpu as pltpu
from jax.sharding import PartitionSpec as P

IRREPS = 8
CD_TILE = 128
ROW_TILE = 8
TILES = 128
KT = 16
OWN_TILES = 8
SLOTS = 32
CAP = 16
VB = 100
VP = 104
ZEROT = 128
DUMPT = 129
PT = 136
T_LST = 0
T_OFF = 1024
T_KL = 1152
T_SRC = 1280
T_NR = 1536
T_NK = 1544
T_FIT = 1552
T_NO = 1560
T_SIZE = 2048

MESH = pl.DeviceIdType.MESH
F32 = jnp.float32
BF16 = jnp.bfloat16


def prep_kernel(row, cd, own, amp, comp, tab):
    me = lax.axis_index("blk")
    for i in range(IRREPS):
        tab[T_NR + i] = 0
        tab[T_NK + i] = 0
    for i in range(16):
        tab[T_NO + i] = 0
    for k in range(KT):
        lab = cd[k]
        kap = tab[T_NK + lab]
        tab[T_KL + lab * KT + kap] = k
        tab[T_NK + lab] = kap + 1
    labs = [cd[k] for k in range(KT)]
    j = jnp.int32(0)
    for t in range(OWN_TILES):
        lab = row[me * OWN_TILES + t]
        for k in range(KT):
            jc = jnp.minimum(j, SLOTS)
            comp[pl.ds(pl.multiple_of(jc * 8, 8), 8), :] = amp[t * 8:(t + 1) * 8, k * 128:(k + 1) * 128]
            j = j + jnp.where(labs[k] == lab, 1, 0)

    def clear(i, c):
        tab[T_SRC + i] = ZEROT
        return c

    lax.fori_loop(0, 256, clear, 0, unroll=16)

    def group(g, most):
        acc = jnp.int32(0)
        for t in range(OWN_TILES):
            r = g * OWN_TILES + t
            lab = row[r]
            p = tab[T_NR + lab]
            tab[T_LST + lab * TILES + p] = r
            tab[T_NR + lab] = p + 1
            o = own[r]
            q = tab[T_NO + o]
            tab[T_SRC + o * CAP + q] = r
            tab[T_NO + o] = q + 1
            tab[T_OFF + r] = g * SLOTS + acc
            acc = acc + tab[T_NK + lab]
        return jnp.maximum(most, acc)

    most = lax.fori_loop(0, TILES // OWN_TILES, group, jnp.int32(0))
    tab[T_FIT] = jnp.where(most <= SLOTS, 1, 0)


def prep(row, cd, own, amp):
    smem = pl.BlockSpec(memory_space=pltpu.SMEM)
    vmem = pl.BlockSpec(memory_space=pltpu.VMEM)
    return pl.pallas_call(
        prep_kernel,
        out_shape=(
            jax.ShapeDtypeStruct(((SLOTS + 1) * 8, 128), F32),
            jax.ShapeDtypeStruct((T_SIZE,), jnp.int32),
        ),
        in_specs=[smem, smem, smem, vmem],
        out_specs=(vmem, smem),
        name="prep",
    )(row, cd, own, amp)


ORDER = (0, 1, 7, 2, 6, 3, 5, 4)


def gather_kernel(cd, airr, comp, integ, g, w, raw, loc_sem, raw_sem, s1, r1, s2, r2, s3, r3):
    slab = lax.axis_index("slab")
    blk = lax.axis_index("blk")
    c = slab % 2
    y = (slab // 2) % 4
    xl = slab // 8
    z = blk // 2
    xh = blk % 2
    x = xh * 2 + xl
    pos = (1 - c) * x + c * y

    def dev(x_, y_, z_, c_):
        return {"slab": (x_ % 2) * 8 + y_ * 2 + c_, "blk": z_ * 2 + x_ // 2}

    raw_copy = pltpu.make_async_copy(integ, raw, raw_sem)
    raw_copy.start()

    col = [dev(x, y, (z + d) % 8, c) for d in range(8)]
    cross = [dev(3 - x, y, (z + d) % 8, c) for d in range(8)]
    ring = [None] + [dev((x + (1 - c) * j) % 4, (y + c * j) % 4, z, c) for j in range(1, 4)]
    twin = dev(x, y, z, 1 - c)

    barrier = pltpu.get_barrier_semaphore()
    peers = col[1:] + cross + ring[1:] + [twin]
    for peer in peers:
        pl.semaphore_signal(barrier, inc=1, device_id=peer, device_id_type=MESH)

    def rows(c_, p_):
        return pl.ds(pl.multiple_of(c_ * 128 + p_ * 32, 32), 32)

    mine = pltpu.make_async_copy(comp.at[rows(c, pos)], g.at[blk, rows(c, pos)], loc_sem)
    mine.start()
    pl.semaphore_wait(barrier, len(peers))

    cross_pos = (1 - c) * (3 - x) + c * y
    first = []
    for d in ORDER:
        if d != 0:
            cp = pltpu.make_async_remote_copy(
                src_ref=comp.at[rows(c, pos)], dst_ref=g.at[blk, rows(c, pos)],
                send_sem=s1.at[0, d], recv_sem=r1.at[0, d],
                device_id=col[d], device_id_type=MESH)
            cp.start()
            first.append(cp)
        cp = pltpu.make_async_remote_copy(
            src_ref=comp.at[rows(c, cross_pos)], dst_ref=g.at[blk, rows(c, cross_pos)],
            send_sem=s1.at[1, d], recv_sem=r1.at[1, d],
            device_id=cross[d], device_id_type=MESH)
        cp.start()
        first.append(cp)

    raw_copy.wait()
    a = airr[slab, blk]

    def weights(k):
        beta = cd[k] ^ a
        odd = beta & 1
        start = beta * 12 + beta // 2
        block = jnp.concatenate([raw[start + i, :, k * 128:(k + 1) * 128] for i in range(VP // 8)], axis=0)
        moved = jnp.concatenate([block[4:], block[:4]], axis=0)
        block = jnp.where(odd == 1, moved, block)
        block = jnp.concatenate([block, jnp.zeros((128 - VP, 128), F32)], axis=0)
        hi = block.astype(BF16)
        lo = (block - hi.astype(F32)).astype(BF16)
        w[k, 0:128, :] = hi
        w[k, 128:256, :] = lo

    def recv_first(d):
        zz = (z + 8 - d) % 8
        if d != 0:
            pltpu.make_async_remote_copy(
                src_ref=comp.at[rows(c, pos)], dst_ref=g.at[zz * 2 + xh, rows(c, pos)],
                send_sem=s1.at[0, d], recv_sem=r1.at[0, d],
                device_id=col[d], device_id_type=MESH).wait_recv()
        pltpu.make_async_remote_copy(
            src_ref=comp.at[rows(c, pos)], dst_ref=g.at[zz * 2 + 1 - xh, rows(c, pos)],
            send_sem=s1.at[1, d], recv_sem=r1.at[1, d],
            device_id=cross[d], device_id_type=MESH).wait_recv()

    later = []
    for i, d in enumerate(ORDER):
        weights(2 * i)
        weights(2 * i + 1)
        if d == 0:
            mine.wait()
        recv_first(d)
        zz = (z + 8 - d) % 8
        part = g.at[pl.ds(zz * 2, 2), rows(c, pos)]
        for j in (2, 1, 3):
            cp = pltpu.make_async_remote_copy(
                src_ref=part, dst_ref=part, send_sem=s2.at[j, d], recv_sem=r2.at[j, d],
                device_id=ring[j], device_id_type=MESH)
            cp.start()
            later.append(cp)
        cp = pltpu.make_async_remote_copy(
            src_ref=part, dst_ref=part, send_sem=s3.at[0, d], recv_sem=r3.at[0, d],
            device_id=twin, device_id_type=MESH)
        cp.start()
        later.append(cp)

    for d in ORDER:
        zz = (z + 8 - d) % 8
        for j in (1, 3, 2):
            part = g.at[pl.ds(zz * 2, 2), rows(c, (pos + 4 - j) % 4)]
            pltpu.make_async_remote_copy(
                src_ref=part, dst_ref=part, send_sem=s2.at[j, d], recv_sem=r2.at[j, d],
                device_id=ring[j], device_id_type=MESH).wait_recv()
            cp = pltpu.make_async_remote_copy(
                src_ref=part, dst_ref=part, send_sem=s3.at[j, d], recv_sem=r3.at[j, d],
                device_id=twin, device_id_type=MESH)
            cp.start()
            later.append(cp)
    other_pos = c * x + (1 - c) * y
    for d in ORDER:
        zz = (z + 8 - d) % 8
        for j in range(4):
            part = g.at[pl.ds(zz * 2, 2), rows(1 - c, (other_pos + 4 - j) % 4)]
            pltpu.make_async_remote_copy(
                src_ref=part, dst_ref=part, send_sem=s3.at[j, d], recv_sem=r3.at[j, d],
                device_id=twin, device_id_type=MESH).wait_recv()
    for cp in first + later:
        cp.wait_send()


def gather(cd, airr, comp, integ):
    smem = pl.BlockSpec(memory_space=pltpu.SMEM)
    vmem = pl.BlockSpec(memory_space=pltpu.VMEM)
    hbm = pl.BlockSpec(memory_space=pl.ANY)
    dma = pltpu.SemaphoreType.DMA
    return pl.pallas_call(
        gather_kernel,
        out_shape=(
            jax.ShapeDtypeStruct((16, SLOTS * 8, 128), F32),
            jax.ShapeDtypeStruct((KT, 256, 128), BF16),
        ),
        in_specs=[smem, smem, vmem, hbm],
        out_specs=(vmem, vmem),
        scratch_shapes=[
            pltpu.VMEM((IRREPS * VB // 8, 8, KT * CD_TILE), F32),
            dma, dma, dma((2, 8)), dma((2, 8)), dma((4, 8)), dma((4, 8)), dma((4, 8)), dma((4, 8)),
        ],
        compiler_params=pltpu.CompilerParams(
            collective_id=0, has_side_effects=True, vmem_limit_bytes=24 * 2**20),
        name="gather",
    )(cd, airr, comp, integ)


def product_kernel(tab, g, w, p, lhs, acc):
    p[ZEROT] = jnp.zeros((8, 128), F32)

    def label(lab, c):
        nr = tab[T_NR + lab]
        nk = tab[T_NK + lab]

        def rowsof(m, c):
            tiles = []
            for t in range(16):
                ok = m * 16 + t < nr
                r = jnp.where(ok, tab[T_LST + lab * TILES + jnp.minimum(m * 16 + t, nr - 1)], 0)
                tiles.append((ok, r, tab[T_OFF + r]))
            acc[...] = jnp.zeros_like(acc)

            def depth(kc, c):
                two = kc * 2 + 1 < nk
                k0 = tab[T_KL + lab * KT + kc * 2]
                k1 = tab[T_KL + lab * KT + jnp.where(two, kc * 2 + 1, kc * 2)]
                for t in range(16):
                    off = tiles[t][2] + kc * 2
                    lhs[t * 8:(t + 1) * 8, 0:128] = g[off]
                    off1 = jnp.where(two, off + 1, off)
                    lhs[t * 8:(t + 1) * 8, 128:256] = jnp.where(two, g[off1], 0.0)
                a = lhs[...]
                hi = a.astype(BF16)
                lo = (a - hi.astype(F32)).astype(BF16)
                ww = jnp.concatenate([w[k0], w[k1]], axis=1)
                nt = (((1,), (1,)), ((), ()))
                big = lax.dot_general(hi, ww, nt, preferred_element_type=F32)
                small = lax.dot_general(lo, ww[:128], nt, preferred_element_type=F32)
                acc[...] += big[:, :128] + (big[:, 128:] + small)
                return c

            lax.fori_loop(0, (nk + 1) // 2, depth, 0)
            for t in range(16):
                ok, r, _ = tiles[t]
                p[jnp.where(ok, r, DUMPT)] = acc[t * 8:(t + 1) * 8, :]
            return c

        return lax.fori_loop(0, (nr + 15) // 16, rowsof, c)

    lax.fori_loop(0, IRREPS, label, 0)


def product(tab, g, w):
    smem = pl.BlockSpec(memory_space=pltpu.SMEM)
    vmem = pl.BlockSpec(memory_space=pltpu.VMEM)
    return pl.pallas_call(
        product_kernel,
        out_shape=jax.ShapeDtypeStruct((PT, 8, 128), F32),
        in_specs=[smem, vmem, vmem],
        out_specs=vmem,
        scratch_shapes=[pltpu.VMEM((128, 256), F32), pltpu.VMEM((128, 128), F32)],
        compiler_params=pltpu.CompilerParams(vmem_limit_bytes=24 * 2**20),
        name="product",
    )(tab, g, w)


def owners_kernel(tab, p, out, send, loc_sem, ss, rs):
    me = lax.axis_index("slab")
    barrier = pltpu.get_barrier_semaphore()
    for i in range(1, 16):
        pl.semaphore_signal(barrier, inc=1, device_id={"slab": (me + i) % 16}, device_id_type=MESH)
    copies = []
    for i in list(range(1, 16)) + [0]:
        o = (me + i) % 16
        block = jnp.concatenate([p[tab[T_SRC + o * CAP + q]] for q in range(CAP)], axis=0)
        send[i] = jnp.transpose(block)[:VP]
        if i == 1:
            pl.semaphore_wait(barrier, 15)
        if i == 0:
            cp = pltpu.make_async_copy(send.at[i], out.at[me], loc_sem)
        else:
            cp = pltpu.make_async_remote_copy(
                src_ref=send.at[i], dst_ref=out.at[me], send_sem=ss.at[i], recv_sem=rs.at[i],
                device_id={"slab": o}, device_id_type=MESH)
        cp.start()
        copies.append(cp)
    for i in range(1, 16):
        src = (me + 16 - i) % 16
        pltpu.make_async_remote_copy(
            src_ref=send.at[i], dst_ref=out.at[src], send_sem=ss.at[i], recv_sem=rs.at[i],
            device_id={"slab": (me + i) % 16}, device_id_type=MESH).wait_recv()
    for cp in copies[:-1]:
        cp.wait_send()
    copies[-1].wait()


def owners(tab, p):
    smem = pl.BlockSpec(memory_space=pltpu.SMEM)
    vmem = pl.BlockSpec(memory_space=pltpu.VMEM)
    dma = pltpu.SemaphoreType.DMA
    return pl.pallas_call(
        owners_kernel,
        out_shape=jax.ShapeDtypeStruct((16, VP, 128), F32),
        in_specs=[smem, vmem],
        out_specs=vmem,
        scratch_shapes=[pltpu.VMEM((16, VP, 128), F32), dma, dma((16,)), dma((16,))],
        compiler_params=pltpu.CompilerParams(
            collective_id=1, has_side_effects=True, vmem_limit_bytes=24 * 2**20),
        name="owners",
    )(tab, p)


def expand_kernel(tab, row, airr, arrived, out):
    s = pl.program_id(0)
    me = lax.axis_index("slab")
    a = airr[s, lax.axis_index("blk")]
    lane = lax.broadcasted_iota(jnp.int32, (1, 128), 1) // 8
    want = jnp.full((1, 128), -1, jnp.int32)
    for q in range(CAP):
        r = tab[T_SRC + me * CAP + q]
        beta = jnp.where(r < TILES, row[jnp.minimum(r, TILES - 1)] ^ a, -1)
        want = jnp.where(lane == q, beta, want)
    block = arrived[0, :VB, :]
    for beta in range(IRREPS):
        out[0, beta * VB:(beta + 1) * VB, :] = jnp.where(want == beta, block, 0.0)


def expand(tab, row, airr, arrived):
    smem = pl.BlockSpec(memory_space=pltpu.SMEM)
    return pl.pallas_call(
        expand_kernel,
        grid=(16,),
        out_shape=jax.ShapeDtypeStruct((16, IRREPS * VB, 128), F32),
        in_specs=[smem, smem, smem, pl.BlockSpec((1, VP, 128), lambda s: (s, 0, 0))],
        out_specs=pl.BlockSpec((1, IRREPS * VB, 128), lambda s: (s, 0, 0)),
        name="expand",
    )(tab, row, airr, arrived)


def dense(amplitude, integ, row, cd, airr, tab):
    slab = lax.axis_index("slab")
    blk = lax.axis_index("blk")
    own_a = airr[slab, blk]
    piece = lax.all_gather(amplitude, "blk", axis=0, tiled=True)
    cd_cols = jnp.repeat(cd, CD_TILE)
    labels = jnp.repeat(row, ROW_TILE)
    coupled = jnp.where(labels[:, None] == cd_cols[None, :], piece, 0.0)
    blocks = integ.reshape(IRREPS, VB, KT * CD_TILE)
    want = cd_cols ^ own_a
    kept = jnp.sum(jnp.where(want[None, None, :] == jnp.arange(IRREPS)[:, None, None], blocks, 0.0), axis=0)
    prod = jnp.dot(coupled, kept.T, precision=lax.Precision.HIGHEST, preferred_element_type=F32)
    prod = jnp.concatenate([prod.reshape(TILES, ROW_TILE, VB), jnp.zeros((1, ROW_TILE, VB), F32)], axis=0)
    packed = jnp.take(prod, tab[T_SRC:T_SRC + 256], axis=0).reshape(16, CAP * ROW_TILE, VB)
    arrived = lax.all_to_all(packed, "slab", split_axis=0, concat_axis=0, tiled=True)
    arrived = jnp.transpose(arrived, (0, 2, 1))
    return jnp.pad(arrived, ((0, 0), (0, VP - VB), (0, 0)))


def shards(amplitude, integrals, row, cd, airr, owner):
    integ = integrals.reshape(KT * CD_TILE, IRREPS * VB).T
    own = owner.reshape(TILES)
    comp, tab = prep(row, cd, own, amplitude)

    def fast(amplitude, integ, row, cd, airr, tab, comp):
        g, w = gather(cd, airr, comp, integ.reshape(IRREPS * VB // 8, 8, KT * CD_TILE))
        p = product(tab, g.reshape(16 * SLOTS, 8, 128), w)
        return owners(tab, p)

    def slow(amplitude, integ, row, cd, airr, tab, comp):
        return dense(amplitude, integ, row, cd, airr, tab)

    arrived = lax.cond(tab[T_FIT] == 1, fast, slow, amplitude, integ, row, cd, airr, tab, comp)
    out = expand(tab, row, airr, arrived)
    return jnp.transpose(out, (2, 0, 1)).reshape(CAP * ROW_TILE, 16, 1, IRREPS * VB)


def solution(mesh):
    return jax.shard_map(
        shards,
        mesh=mesh,
        in_specs=(P("blk", None), P(None, "slab", "blk", None), P(), P(), P(), P()),
        out_specs=P("slab", None, "blk", None),
        check_vma=False,
    )
```

time: 231 us -> 75.4 us (0.33)
  waiting for transfers between devices: 133 us -> 0 us
  Pallas kernels: 0 us -> 60.1 us
  matrix products: 31.2 us -> 0 us
  local copies, waits for them, and re-layouts: 28.2 us -> 0.58 us
  other arithmetic: 19.3 us -> 0 us
  starting transfers between devices: 5.39 us -> 0 us
    all_gather x1 -> x0, waiting for transfers between devices: 118 us -> none  [shards(): piece = lax.all_gather(amplitude, 'blk', axis=0, tiled=True)]
    pallas_call x0 -> x5, Pallas kernels: none -> 60.1 us  [the longest x1 26.9 us: gather(): pl.pallas_call(gather_kernel, out_shape=(jax.ShapeDtypeStruct((16, SLOTS...]
    dot_general x2 -> x0, matrix products: 31.2 us -> none  [the longest x1 30.6 us: shards(): jnp.dot(coupled, flat, precision=lax.Precision.HIGHEST, preferred_element...]
    all_to_all x1 -> x0, waiting for transfers between devices: 14.6 us -> none  [shards(): lax.all_to_all(packed, 'slab', split_axis=0, concat_axis=1, tiled=True)]
    gather x3 -> x0, local copies, waits for them, and re-layouts: 8.47 us -> none  [the longest x1 5.85 us: shards(): labels = jnp.take(row_irrep, rows)]
    select_n x2 -> x0, local copies, waits for them, and re-layouts: 8.1 us -> none  [the longest x1 4.79 us: shards(): expanded = jnp.where(place, arrived[:, :, :, None, :], 0.0)]
    reshape x3 -> x0, local copies, waits for them, and re-layouts: 7.3 us -> none  [the longest x1 5.58 us: shards(): split_blocks = ladder.reshape(tiles, ROW_TILE, a_count, IRREPS, vblock)]
    select_n x6 -> x0, other arithmetic: 6.3 us -> none  [the longest x1 5.57 us: shards(): jnp.take(cd_irrep, jnp.arange(cdpairs, dtype=jnp.int32) // CD_TILE)]
  transfers between devices with their start and end apart: 2 -> 0, of which waited for: 2 -> 0; matrix products, arithmetic and copies ran while one was open for 11% -> 0% of each run, Pallas kernels for 0% -> 0%
where the time goes in v1:
time: 75.4 us; the launch traced here: 74.7 us
  Pallas kernels  60.1 us (80%)
  between operations  14 us (19%)
    pallas_call x1, Pallas kernels, gather(): pl.pallas_call(gather_kernel, out_shape=(jax.ShapeDtypeStruct((16, SLOTS...  26.9 us
    pallas_call x1, Pallas kernels, owners(): pl.pallas_call(owners_kernel, out_shape=jax.ShapeDtypeStruct((16, VP, 128...  16.1 us
    pallas_call x1, Pallas kernels, expand(): pl.pallas_call(expand_kernel, grid=(16,), out_shape=jax.ShapeDtypeStruct(...  7.81 us
    pallas_call x1, Pallas kernels, product(): pl.pallas_call(product_kernel, out_shape=jax.ShapeDtypeStruct((PT, 8, 128...  5.17 us
    pallas_call x1, Pallas kernels, prep(): pl.pallas_call(prep_kernel, out_shape=(jax.ShapeDtypeStruct(((SLOTS + 1)...  4.11 us

profile of v1, /device:TPU:1, one launch (start us, length us, event | category | flops | bytes accessed | tf_op | source)
XLA Modules:
  0.0 74.7 jit_solution(12200451079826326662)
XLA Ops:
  6.5 4.1 %prep.1 = (f32[264,128]{1,0:T(8,128)S(1)}, s32[2048]{0:T(1024)S(1)}) custom-call(s32[128]{0:T(128)} %row.3, s32[16]{0:T(128)} %cd.1, s32[128]{0:T(128)} %bitcast.34, f32[64,2048]{1,0:T(8,128)} %amp.1), custom_call_target="tpu_custom_call" | custom-call | tf_op jit(solution)/shard_map/prep/pallas_call | solution.py:88
  10.7 0.6 slice.14
  11.9 48.2 %conditional.1 = (f32[16,104,128]{2,1,0:T(8,128)S(1)}) conditional(s32[]{:T(128)} %bitcast.10, (s32[2048]{0:T(1024)S(1)}, s32[128]{0:T(128)}, s32[16]{0:T(128)}, f32[64,2048]{1,0:T(8,128)}, s32[16,16]{1,0:T(8,128)}, /*index=5*/f32[800,2048]{1,0:T(8,128)}) %tuple.18, (f32[800,2048]{1,0:T(8,128)}, s32[16]{0:T(128)}, s32[16,16]{1,0:T(8,128)}, ...), branch_computations={%region_0.2_spmd, %region_2.3_spmd} | conditional | flops 2524075264 | bytes 65989876 | solution.py:414
  11.9 26.9 %gather.9 = (f32[16,256,128]{2,1,0:T(8,128)S(1)}, bf16[16,256,128]{2,1,0:T(8,128)(2,1)S(1)}) custom-call(s32[16]{0:T(128)} %get-tuple-element.37.cd, s32[16,16]{1,0:T(8,128)} %get-tuple-element.38.airr, f32[264,128]{1,0:T(8,128)S(1)} %get-tuple-element.39.comp, f32[100,8,2048]{2,1,0:T(8,128)} %bitcast.31), custom_call_target="tpu_custom_call" | custom-call | tf_op jit(solution)/shard_map/cond/branch_1_fun/gather/pallas_call | solution.py:232
  38.8 5.2 %product.1.p = f32[136,8,128]{2,1,0:T(8,128)S(1)} custom-call(s32[2048]{0:T(1024)S(1)} %get-tuple-element.36.tab, f32[512,8,128]{2,1,0:T(8,128)S(1)} %bitcast.28, bf16[16,256,128]{2,1,0:T(8,128)(2,1)S(1)} %get-tuple-element.42.w), custom_call_target="tpu_custom_call" | custom-call | tf_op jit(solution)/shard_map/cond/branch_1_fun/product/pallas_call | solution.py:298
  44.0 16.1 %owners.1 = f32[16,104,128]{2,1,0:T(8,128)S(1)} custom-call(s32[2048]{0:T(1024)S(1)} %get-tuple-element.36.tab, f32[136,8,128]{2,1,0:T(8,128)S(1)} %product.1.p), custom_call_target="tpu_custom_call" | custom-call | tf_op jit(solution)/shard_map/cond/branch_1_fun/owners/pallas_call | solution.py:343
  60.1 7.8 %expand.1 = f32[16,800,128]{2,1,0:T(8,128)} custom-call(s32[2048]{0:T(1024)S(1)} %get-tuple-element.45.tab, s32[128]{0:T(128)} %row.3, s32[16,16]{1,0:T(8,128)} %airr.1, f32[16,104,128]{2,1,0:T(8,128)S(1)} %get-tuple-element.49.arrived), custom_call_target="tpu_custom_call" | custom-call | tf_op jit(solution)/shard_map/expand/pallas_call | solution.py:372

commit v2 on v1

--- a/solution.py
+++ b/solution.py
@@ -20,69 +20,84 @@
 ZEROT = 128
 DUMPT = 129
 PT = 136
+MT = 24
 T_LST = 0
-T_OFF = 1024
-T_KL = 1152
-T_SRC = 1280
-T_NR = 1536
-T_NK = 1544
-T_FIT = 1552
-T_NO = 1560
-T_SIZE = 2048
+T_KL = 1024
+T_SRC = 1152
+T_NR = 1408
+T_NK = 1416
+T_FIT = 1424
+T_BETA = 1440
+T_A = 1456
+T_LAB = 1472
+T_NO = 1488
+T_SIZE = 1536
 
 MESH = pl.DeviceIdType.MESH
 F32 = jnp.float32
 BF16 = jnp.bfloat16
 
 
-def prep_kernel(row, cd, own, amp, comp, tab):
-    me = lax.axis_index("blk")
+def prep_kernel(row, cd, airr, own, amp_hbm, comp, tab, amp, amp_sem):
+    slab = lax.axis_index("slab")
+    blk = lax.axis_index("blk")
+    load = pltpu.make_async_copy(amp_hbm, amp, amp_sem)
+    load.start()
     for i in range(IRREPS):
         tab[T_NR + i] = 0
         tab[T_NK + i] = 0
     for i in range(16):
         tab[T_NO + i] = 0
+    labs = [cd[k] for k in range(KT)]
+    mine = airr[slab, blk]
     for k in range(KT):
-        lab = cd[k]
+        lab = labs[k]
         kap = tab[T_NK + lab]
         tab[T_KL + lab * KT + kap] = k
         tab[T_NK + lab] = kap + 1
-    labs = [cd[k] for k in range(KT)]
+        tab[T_BETA + k] = lab ^ mine
+    for i in range(16):
+        tab[T_A + i] = airr[i, blk]
+
+    def clear(i, c):
+        for u in range(32):
+            tab[T_SRC + i * 32 + u] = ZEROT
+        return c
+
+    lax.fori_loop(0, 8, clear, 0)
+
+    def group(g, most):
+        rs = [g * OWN_TILES + t for t in range(OWN_TILES)]
+        ls = [row[r] for r in rs]
+        os = [own[r] for r in rs]
+        ks = [tab[T_NK + lab] for lab in ls]
+        acc = g * SLOTS
+        for r, lab, o, kn in zip(rs, ls, os, ks):
+            p = tab[T_NR + lab]
+            q = tab[T_NO + o]
+            tab[T_LST + lab * TILES + p] = r + acc * 256
+            tab[T_NR + lab] = p + 1
+            tab[T_SRC + o * CAP + q] = r
+            tab[T_NO + o] = q + 1
+            acc = acc + kn
+        return jnp.maximum(most, acc - g * SLOTS)
+
+    most = lax.fori_loop(0, TILES // OWN_TILES, group, jnp.int32(0))
+    tab[T_FIT] = jnp.where(most <= SLOTS, 1, 0)
+    for q in range(CAP):
+        tab[T_LAB + q] = row[jnp.minimum(tab[T_SRC + slab * CAP + q], TILES - 1)]
+
+    load.wait()
     j = jnp.int32(0)
     for t in range(OWN_TILES):
-        lab = row[me * OWN_TILES + t]
+        lab = row[blk * OWN_TILES + t]
         for k in range(KT):
             jc = jnp.minimum(j, SLOTS)
             comp[pl.ds(pl.multiple_of(jc * 8, 8), 8), :] = amp[t * 8:(t + 1) * 8, k * 128:(k + 1) * 128]
             j = j + jnp.where(labs[k] == lab, 1, 0)
 
-    def clear(i, c):
-        tab[T_SRC + i] = ZEROT
-        return c
-
-    lax.fori_loop(0, 256, clear, 0, unroll=16)
-
-    def group(g, most):
-        acc = jnp.int32(0)
-        for t in range(OWN_TILES):
-            r = g * OWN_TILES + t
-            lab = row[r]
-            p = tab[T_NR + lab]
-            tab[T_LST + lab * TILES + p] = r
-            tab[T_NR + lab] = p + 1
-            o = own[r]
-            q = tab[T_NO + o]
-            tab[T_SRC + o * CAP + q] = r
-            tab[T_NO + o] = q + 1
-            tab[T_OFF + r] = g * SLOTS + acc
-            acc = acc + tab[T_NK + lab]
-        return jnp.maximum(most, acc)
-
-    most = lax.fori_loop(0, TILES // OWN_TILES, group, jnp.int32(0))
-    tab[T_FIT] = jnp.where(most <= SLOTS, 1, 0)
-
-
-def prep(row, cd, own, amp):
+
+def prep(row, cd, airr, own, amp):
     smem = pl.BlockSpec(memory_space=pltpu.SMEM)
     vmem = pl.BlockSpec(memory_space=pltpu.VMEM)
     return pl.pallas_call(
@@ -91,16 +106,18 @@
             jax.ShapeDtypeStruct(((SLOTS + 1) * 8, 128), F32),
             jax.ShapeDtypeStruct((T_SIZE,), jnp.int32),
         ),
-        in_specs=[smem, smem, smem, vmem],
+        in_specs=[smem, smem, smem, smem, pl.BlockSpec(memory_space=pl.ANY)],
         out_specs=(vmem, smem),
+        scratch_shapes=[pltpu.VMEM((OWN_TILES * 8, KT * CD_TILE), F32), pltpu.SemaphoreType.DMA],
+        compiler_params=pltpu.CompilerParams(vmem_limit_bytes=50 * 2**20),
         name="prep",
-    )(row, cd, own, amp)
+    )(row, cd, airr, own, amp)
 
 
 ORDER = (0, 1, 7, 2, 6, 3, 5, 4)
 
 
-def gather_kernel(cd, airr, comp, integ, g, w, raw, loc_sem, raw_sem, s1, r1, s2, r2, s3, r3):
+def gather_kernel(tab, comp, integ, g, w, raw, loc_sem, raw_sem, s1, r1, s2, r2, s3, r3):
     slab = lax.axis_index("slab")
     blk = lax.axis_index("blk")
     c = slab % 2
@@ -152,10 +169,9 @@
         first.append(cp)
 
     raw_copy.wait()
-    a = airr[slab, blk]
 
     def weights(k):
-        beta = cd[k] ^ a
+        beta = tab[T_BETA + k]
         odd = beta & 1
         start = beta * 12 + beta // 2
         block = jnp.concatenate([raw[start + i, :, k * 128:(k + 1) * 128] for i in range(VP // 8)], axis=0)
@@ -224,7 +240,7 @@
         cp.wait_send()
 
 
-def gather(cd, airr, comp, integ):
+def gather(tab, comp, integ):
     smem = pl.BlockSpec(memory_space=pltpu.SMEM)
     vmem = pl.BlockSpec(memory_space=pltpu.VMEM)
     hbm = pl.BlockSpec(memory_space=pl.ANY)
@@ -235,7 +251,7 @@
             jax.ShapeDtypeStruct((16, SLOTS * 8, 128), F32),
             jax.ShapeDtypeStruct((KT, 256, 128), BF16),
         ),
-        in_specs=[smem, smem, vmem, hbm],
+        in_specs=[smem, vmem, hbm],
         out_specs=(vmem, vmem),
         scratch_shapes=[
             pltpu.VMEM((IRREPS * VB // 8, 8, KT * CD_TILE), F32),
@@ -244,7 +260,7 @@
         compiler_params=pltpu.CompilerParams(
             collective_id=0, has_side_effects=True, vmem_limit_bytes=24 * 2**20),
         name="gather",
-    )(cd, airr, comp, integ)
+    )(tab, comp, integ)
 
 
 def product_kernel(tab, g, w, p, lhs, acc):
@@ -256,18 +272,18 @@
 
         def rowsof(m, c):
             tiles = []
-            for t in range(16):
-                ok = m * 16 + t < nr
-                r = jnp.where(ok, tab[T_LST + lab * TILES + jnp.minimum(m * 16 + t, nr - 1)], 0)
-                tiles.append((ok, r, tab[T_OFF + r]))
+            for t in range(MT):
+                ok = m * MT + t < nr
+                v = tab[T_LST + lab * TILES + jnp.minimum(m * MT + t, nr - 1)]
+                tiles.append((jnp.where(ok, v & 255, DUMPT), v >> 8))
             acc[...] = jnp.zeros_like(acc)
 
             def depth(kc, c):
                 two = kc * 2 + 1 < nk
                 k0 = tab[T_KL + lab * KT + kc * 2]
                 k1 = tab[T_KL + lab * KT + jnp.where(two, kc * 2 + 1, kc * 2)]
-                for t in range(16):
-                    off = tiles[t][2] + kc * 2
+                for t in range(MT):
+                    off = tiles[t][1] + kc * 2
                     lhs[t * 8:(t + 1) * 8, 0:128] = g[off]
                     off1 = jnp.where(two, off + 1, off)
                     lhs[t * 8:(t + 1) * 8, 128:256] = jnp.where(two, g[off1], 0.0)
@@ -282,12 +298,11 @@
                 return c
 
             lax.fori_loop(0, (nk + 1) // 2, depth, 0)
-            for t in range(16):
-                ok, r, _ = tiles[t]
-                p[jnp.where(ok, r, DUMPT)] = acc[t * 8:(t + 1) * 8, :]
+            for t in range(MT):
+                p[tiles[t][0]] = acc[t * 8:(t + 1) * 8, :]
             return c
 
-        return lax.fori_loop(0, (nr + 15) // 16, rowsof, c)
+        return lax.fori_loop(0, (nr + MT - 1) // MT, rowsof, c)
 
     lax.fori_loop(0, IRREPS, label, 0)
 
@@ -300,7 +315,7 @@
         out_shape=jax.ShapeDtypeStruct((PT, 8, 128), F32),
         in_specs=[smem, vmem, vmem],
         out_specs=vmem,
-        scratch_shapes=[pltpu.VMEM((128, 256), F32), pltpu.VMEM((128, 128), F32)],
+        scratch_shapes=[pltpu.VMEM((MT * 8, 256), F32), pltpu.VMEM((MT * 8, 128), F32)],
         compiler_params=pltpu.CompilerParams(vmem_limit_bytes=24 * 2**20),
         name="product",
     )(tab, g, w)
@@ -352,38 +367,51 @@
     )(tab, p)
 
 
-def expand_kernel(tab, row, airr, arrived, out):
-    s = pl.program_id(0)
-    me = lax.axis_index("slab")
-    a = airr[s, lax.axis_index("blk")]
+def expand_kernel(tab, arrived, out, stage, sems):
     lane = lax.broadcasted_iota(jnp.int32, (1, 128), 1) // 8
-    want = jnp.full((1, 128), -1, jnp.int32)
+    lab = jnp.zeros((1, 128), jnp.int32)
     for q in range(CAP):
-        r = tab[T_SRC + me * CAP + q]
-        beta = jnp.where(r < TILES, row[jnp.minimum(r, TILES - 1)] ^ a, -1)
-        want = jnp.where(lane == q, beta, want)
-    block = arrived[0, :VB, :]
-    for beta in range(IRREPS):
-        out[0, beta * VB:(beta + 1) * VB, :] = jnp.where(want == beta, block, 0.0)
-
-
-def expand(tab, row, airr, arrived):
-    smem = pl.BlockSpec(memory_space=pltpu.SMEM)
+        lab = jnp.where(lane == q, tab[T_LAB + q], lab)
+    upper = lax.broadcasted_iota(jnp.int32, (8, 128), 0) < 4
+
+    def one(s, c):
+        want = lab ^ tab[T_A + s]
+        block = arrived[s]
+        moved = jnp.concatenate([block[100:104], block[0:100]], axis=0)
+        for m in range(IRREPS // 2):
+            even = want == 2 * m
+            odd = want == 2 * m + 1
+            base = 2 * VB * m
+            stage[s, base:base + 96, :] = jnp.where(even, block[:96], 0.0)
+            stage[s, base + 96:base + 104, :] = jnp.where(
+                upper, jnp.where(even, block[96:], 0.0), jnp.where(odd, moved[:8], 0.0))
+            stage[s, base + 104:base + 200, :] = jnp.where(odd, moved[8:], 0.0)
+        pltpu.make_async_copy(stage.at[s], out.at[s], sems.at[s]).start()
+        return c
+
+    lax.fori_loop(0, 16, one, 0)
+    for s in range(16):
+        pltpu.make_async_copy(stage.at[s], out.at[s], sems.at[s]).wait()
+
+
+def expand(tab, arrived):
     return pl.pallas_call(
         expand_kernel,
-        grid=(16,),
         out_shape=jax.ShapeDtypeStruct((16, IRREPS * VB, 128), F32),
-        in_specs=[smem, smem, smem, pl.BlockSpec((1, VP, 128), lambda s: (s, 0, 0))],
-        out_specs=pl.BlockSpec((1, IRREPS * VB, 128), lambda s: (s, 0, 0)),
+        in_specs=[pl.BlockSpec(memory_space=pltpu.SMEM), pl.BlockSpec(memory_space=pltpu.VMEM)],
+        out_specs=pl.BlockSpec(memory_space=pl.ANY),
+        scratch_shapes=[pltpu.VMEM((16, IRREPS * VB, 128), F32), pltpu.SemaphoreType.DMA((16,))],
+        compiler_params=pltpu.CompilerParams(vmem_limit_bytes=40 * 2**20),
         name="expand",
-    )(tab, row, airr, arrived)
+    )(tab, arrived)
 
 
 def dense(amplitude, integ, row, cd, airr, tab):
     slab = lax.axis_index("slab")
     blk = lax.axis_index("blk")
     own_a = airr[slab, blk]
-    piece = lax.all_gather(amplitude, "blk", axis=0, tiled=True)
+    copies = jnp.broadcast_to(amplitude[None], (16,) + amplitude.shape)
+    piece = lax.all_to_all(copies, "blk", split_axis=0, concat_axis=0, tiled=True).reshape(-1, KT * CD_TILE)
     cd_cols = jnp.repeat(cd, CD_TILE)
     labels = jnp.repeat(row, ROW_TILE)
     coupled = jnp.where(labels[:, None] == cd_cols[None, :], piece, 0.0)
@@ -401,10 +429,10 @@
 def shards(amplitude, integrals, row, cd, airr, owner):
     integ = integrals.reshape(KT * CD_TILE, IRREPS * VB).T
     own = owner.reshape(TILES)
-    comp, tab = prep(row, cd, own, amplitude)
+    comp, tab = prep(row, cd, airr, own, amplitude)
 
     def fast(amplitude, integ, row, cd, airr, tab, comp):
-        g, w = gather(cd, airr, comp, integ.reshape(IRREPS * VB // 8, 8, KT * CD_TILE))
+        g, w = gather(tab, comp, integ.reshape(IRREPS * VB // 8, 8, KT * CD_TILE))
         p = product(tab, g.reshape(16 * SLOTS, 8, 128), w)
         return owners(tab, p)
 
@@ -412,7 +440,7 @@
         return dense(amplitude, integ, row, cd, airr, tab)
 
     arrived = lax.cond(tab[T_FIT] == 1, fast, slow, amplitude, integ, row, cd, airr, tab, comp)
-    out = expand(tab, row, airr, arrived)
+    out = expand(tab, arrived)
     return jnp.transpose(out, (2, 0, 1)).reshape(CAP * ROW_TILE, 16, 1, IRREPS * VB)
 
 

time: 75.4 us -> 56.6 us (0.75)
  between operations: 14 us -> 0.67 us
  Pallas kernels: 60.1 us -> 54 us
    pallas_call x1, Pallas kernels: 7.81 us -> 3.55 us  [expand(): pl.pallas_call(expand_kernel, out_shape=jax.ShapeDtypeStruct((16, IRREPS...]
    pallas_call x1, Pallas kernels: 5.17 us -> 4.11 us  [product(): pl.pallas_call(product_kernel, out_shape=jax.ShapeDtypeStruct((PT, 8, 128...]
where the time goes in v2:
time: 56.6 us; the launch traced here: 56 us
  Pallas kernels  54 us (95%)
  local copies, waits for them, and re-layouts  1.24 us (2%)
  between operations  0.67 us (1%)
    pallas_call x1, Pallas kernels, gather(): pl.pallas_call(gather_kernel, out_shape=(jax.ShapeDtypeStruct((16, SLOTS...  26.7 us
    pallas_call x1, Pallas kernels, owners(): pl.pallas_call(owners_kernel, out_shape=jax.ShapeDtypeStruct((16, VP, 128...  16 us
    pallas_call x1, Pallas kernels, product(): pl.pallas_call(product_kernel, out_shape=jax.ShapeDtypeStruct((PT, 8, 128...  4.11 us
    pallas_call x1, Pallas kernels, prep(): pl.pallas_call(prep_kernel, out_shape=(jax.ShapeDtypeStruct(((SLOTS + 1)...  3.58 us
    pallas_call x1, Pallas kernels, expand(): pl.pallas_call(expand_kernel, out_shape=jax.ShapeDtypeStruct((16, IRREPS...  3.55 us

profile of v2, /device:TPU:1, one launch (start us, length us, event | category | flops | bytes accessed | tf_op | source)
XLA Modules:
  0.0 56.0 jit_solution(6358013200513069592)
XLA Ops:
  0.0 0.0 copy-start
  0.0 0.7 %copy-done = s32[128,1]{0,1:T(1,128)S(1)} copy-done((s32[128,1]{0,1:T(1,128)S(1)}, s32[128,1]{0,1:T(1,128)}, u32[]{:S(2)}) %copy-start) | copy-done | bytes 536
  0.7 3.6 %prep.1 = (f32[264,128]{1,0:T(8,128)S(1)}, s32[1536]{0:T(1024)S(1)}) custom-call(s32[128]{0:T(128)} %row.1, s32[16]{0:T(128)} %cd.1, s32[16,16]{1,0:T(8,128)} %airr.1, s32[128]{0:T(128)S(1)} %bitcast.27, f32[64,2048]{1,0:T(8,128)} %amp_hbm.1), custom_call_target="tpu_custom_call" | custom-call | tf_op jit(solution)/shard_map/prep/pallas_call | solution.py:103
  4.2 0.6 %slice.14 = s32[1]{0:T(128)} slice(s32[1536]{0:T(1024)S(1)} %get-tuple-element.39.tab), slice={[1424:1425]} | slice | bytes 8 | tf_op jit(solution)/shard_map/slice | solution.py:442
  5.5 46.9 %conditional.1 = (f32[16,104,128]{2,1,0:T(8,128)S(1)}) conditional(s32[]{:T(128)} %bitcast.10, (s32[1536]{0:T(1024)S(1)}, s32[128]{0:T(128)}, s32[16]{0:T(128)}, f32[64,2048]{1,0:T(8,128)}, s32[16,16]{1,0:T(8,128)}, /*index=5*/f32[800,2048]{1,0:T(8,128)}) %tuple.16, (f32[800,2048]{1,0:T(8,128)}, s32[1536]{0:T(1024)S(1)}, ...), branch_computations={%region_0.2_spmd, %region_2.3_spmd} | conditional | flops 2524075264 | bytes 73313512 | solution.py:442
  5.5 26.7 %gather.9 = (f32[16,256,128]{2,1,0:T(8,128)S(1)}, bf16[16,256,128]{2,1,0:T(8,128)(2,1)S(1)}) custom-call(s32[1536]{0:T(1024)S(1)} %get-tuple-element.32.tab, f32[264,128]{1,0:T(8,128)S(1)} %get-tuple-element.33.comp, f32[100,8,2048]{2,1,0:T(8,128)} %bitcast.30), custom_call_target="tpu_custom_call" | custom-call | tf_op jit(solution)/shard_map/cond/branch_1_fun/gather/pallas_call | solution.py:248
  32.3 4.1 %product.1.p = f32[136,8,128]{2,1,0:T(8,128)S(1)} custom-call(s32[1536]{0:T(1024)S(1)} %get-tuple-element.32.tab, f32[512,8,128]{2,1,0:T(8,128)S(1)} %bitcast.26, bf16[16,256,128]{2,1,0:T(8,128)(2,1)S(1)} %get-tuple-element.36.w), custom_call_target="tpu_custom_call" | custom-call | tf_op jit(solution)/shard_map/cond/branch_1_fun/product/pallas_call | solution.py:313
  36.4 16.0 %owners.1 = f32[16,104,128]{2,1,0:T(8,128)S(1)} custom-call(s32[1536]{0:T(1024)S(1)} %get-tuple-element.32.tab, f32[136,8,128]{2,1,0:T(8,128)S(1)} %product.1.p), custom_call_target="tpu_custom_call" | custom-call | tf_op jit(solution)/shard_map/cond/branch_1_fun/owners/pallas_call | solution.py:358
  52.4 3.5 %expand.1 = f32[16,800,128]{2,1,0:T(8,128)} custom-call(s32[1536]{0:T(1024)S(1)} %get-tuple-element.39.tab, f32[16,104,128]{2,1,0:T(8,128)S(1)} %get-tuple-element.43.arrived), custom_call_target="tpu_custom_call" | custom-call | tf_op jit(solution)/shard_map/expand/pallas_call | solution.py:398
Async XLA Ops:
  0.0 0.7 %copy-start = (s32[128,1]{0,1:T(1,128)S(1)}, s32[128,1]{0,1:T(1,128)}, u32[]{:S(2)}) copy-start(s32[128,1]{0,1:T(1,128)} %param.13) | copy-start | bytes 1540

commit v3 on v2

v3 whole, which is shorter than its diff:
```python
import functools

import jax
import jax.numpy as jnp
from jax import lax
from jax.experimental import pallas as pl
from jax.experimental.pallas import tpu as pltpu
from jax.sharding import PartitionSpec as P

IRREPS = 8
CD_TILE = 128
ROW_TILE = 8
TILES = 128
KT = 16
OWN_TILES = 8
SLOTS = 32
CAP = 16
VB = 100
VP = 104
ZEROT = 128
DUMPT = 129
PT = 136
MT = 24
KC = 2
T_LST = 0
T_SRC = 1
T_START = 3
T_KL = 4
T_NK = 5
T_LAB = 6

MESH = pl.DeviceIdType.MESH
F32 = jnp.float32
BF16 = jnp.bfloat16


ORDER = (0, 2, 6, 1, 7, 3, 5, 4)


def gather_kernel(row, cd, airr, row_v, own_v, amp_hbm, integ, g, w, tab, fit, comp, found, found_s, raw, amp, amp_sem, found_sem, loc_sem, raw_sem, s1, r1, s2, r2, s3, r3):
    slab = lax.axis_index("slab")
    blk = lax.axis_index("blk")
    c = slab % 2
    y = (slab // 2) % 4
    xl = slab // 8
    z = blk // 2
    xh = blk % 2
    x = xh * 2 + xl
    pos = (1 - c) * x + c * y

    def dev(x_, y_, z_, c_):
        return {"slab": (x_ % 2) * 8 + y_ * 2 + c_, "blk": z_ * 2 + x_ // 2}

    amp_copy = pltpu.make_async_copy(amp_hbm, amp, amp_sem)
    amp_copy.start()
    raw_copy = pltpu.make_async_copy(integ, raw, raw_sem)
    raw_copy.start()

    near = {d: dev(x, y, (z + d) % 8, c) for d in (1, 7, 2, 6)}
    cross = {d: dev(3 - x, y, (z + d) % 8, c) for d in (0, 1, 7, 2, 6)}
    ring = [None] + [dev((x + (1 - c) * j) % 4, (y + c * j) % 4, z, c) for j in range(1, 4)]
    twin = dev(x, y, z, 1 - c)

    barrier = pltpu.get_barrier_semaphore()
    peers = list(near.values()) + list(cross.values()) + ring[1:] + [twin]
    for peer in peers:
        pl.semaphore_signal(barrier, inc=1, device_id=peer, device_id_type=MESH)

    def rows(c_, p_):
        return pl.ds(pl.multiple_of(c_ * 128 + p_ * 32, 32), 32)

    labs = [cd[k] for k in range(KT)]
    sub = lax.broadcasted_iota(jnp.int32, (128, 128), 0)
    lane = lax.broadcasted_iota(jnp.int32, (128, 128), 1)
    one_lane = lax.broadcasted_iota(jnp.int32, (1, 128), 1)

    def coupled_at(place):
        left = jnp.zeros(place.shape, jnp.int32)
        for t in range(OWN_TILES):
            left = jnp.where(place // KT == t, row[blk * OWN_TILES + t], left)
        right = jnp.zeros(place.shape, jnp.int32)
        for k in range(KT):
            right = jnp.where(place % KT == k, labs[k], right)
        return left == right

    down = coupled_at(lax.broadcasted_iota(jnp.int32, (128, 1), 0))
    across = jnp.where(coupled_at(one_lane), 1, 0)
    ahead = jnp.sum(jnp.where(lane < sub, across, 0), axis=1, keepdims=True)
    place = jnp.where(down, ahead, -1)
    found[...] = jnp.sum(jnp.where(place == lane, sub, 0), axis=0, keepdims=True)
    move = pltpu.make_async_copy(found, found_s, found_sem)
    move.start()
    move.wait()
    amp_copy.wait()
    for j in range(SLOTS):
        comp[j * 8:(j + 1) * 8, :] = amp[found_s[0, j]]

    mine = pltpu.make_async_copy(comp.at[rows(c, pos)], g.at[blk, rows(c, pos)], loc_sem)
    mine.start()
    pl.semaphore_wait(barrier, len(peers))

    cross_pos = (1 - c) * (3 - x) + c * y
    first = []
    for d in (2, 6, 0, 1, 7):
        if d != 0:
            cp = pltpu.make_async_remote_copy(
                src_ref=comp.at[rows(c, pos)], dst_ref=g.at[blk, rows(c, pos)],
                send_sem=s1.at[0, d], recv_sem=r1.at[0, d],
                device_id=near[d], device_id_type=MESH)
            cp.start()
            first.append(cp)
        cp = pltpu.make_async_remote_copy(
            src_ref=comp.at[rows(c, cross_pos)], dst_ref=g.at[blk, rows(c, cross_pos)],
            send_sem=s1.at[1, d], recv_sem=r1.at[1, d],
            device_id=cross[d], device_id_type=MESH)
        cp.start()
        first.append(cp)

    row_l = row_v[...]
    own_l = own_v[...]
    diag = sub == lane
    row_c = jnp.sum(jnp.where(diag, row_l, 0), axis=1, keepdims=True)
    own_c = jnp.sum(jnp.where(diag, own_l, 0), axis=1, keepdims=True)
    before = lane < sub
    sub_c = lax.broadcasted_iota(jnp.int32, (128, 1), 0)
    rank = jnp.sum(jnp.where((own_l == own_c) & before, 1, 0), axis=1, keepdims=True)
    target = own_c * CAP + rank
    for h in range(2):
        tab[T_SRC + h:T_SRC + h + 1, :] = ZEROT + jnp.sum(
            jnp.where(target == lane + h * 128, sub - ZEROT, 0), axis=0, keepdims=True)
    tab[T_LAB:T_LAB + 1, :] = jnp.sum(
        jnp.where(target == slab * CAP + lane // ROW_TILE, row_c, 0), axis=0, keepdims=True)
    order = jnp.sum(jnp.where((row_l < row_c) | ((row_l == row_c) & before), 1, 0), axis=1, keepdims=True)
    nk_l = jnp.zeros((1, 128), jnp.int32)
    nk_c = jnp.zeros((128, 1), jnp.int32)
    nk_of = jnp.zeros((1, 128), jnp.int32)
    list_l = jnp.zeros((1, 128), jnp.int32)
    for k in range(KT):
        nk_l = nk_l + jnp.where(row_l == labs[k], 1, 0)
        nk_c = nk_c + jnp.where(row_c == labs[k], 1, 0)
        nk_of = nk_of + jnp.where(one_lane == labs[k], 1, 0)
        kap = jnp.int32(0)
        for other in range(k):
            kap = kap + jnp.where(labs[other] == labs[k], 1, 0)
        list_l = list_l + jnp.where(one_lane == labs[k] * KT + kap, k, 0)
    same = (lane // OWN_TILES == sub // OWN_TILES) & before
    inside = jnp.sum(jnp.where(same, nk_l, 0), axis=1, keepdims=True)
    value = sub_c + 256 * (SLOTS * (sub_c // OWN_TILES) + inside)
    tab[T_LST:T_LST + 1, :] = jnp.sum(jnp.where(order == lane, value, 0), axis=0, keepdims=True)
    tab[T_START:T_START + 1, :] = jnp.sum(jnp.where(row_c < lane, 1, 0), axis=0, keepdims=True)
    tab[T_KL:T_KL + 1, :] = list_l
    tab[T_NK:T_NK + 1, :] = nk_of
    tab[7:8, :] = jnp.zeros((1, 128), jnp.int32)
    fit[0] = jnp.where(jnp.max(inside + nk_c) <= SLOTS, 1, 0)

    raw_copy.wait()
    own_a = airr[slab, blk]

    def weights(k):
        beta = labs[k] ^ own_a
        odd = beta & 1
        start = beta * 12 + beta // 2
        block = jnp.concatenate([raw[start + i, :, k * 128:(k + 1) * 128] for i in range(VP // 8)], axis=0)
        moved = jnp.concatenate([block[4:], block[:4]], axis=0)
        block = jnp.where(odd == 1, moved, block)
        block = jnp.concatenate([block, jnp.zeros((128 - VP, 128), F32)], axis=0)
        hi = block.astype(BF16)
        lo = (block - hi.astype(F32)).astype(BF16)
        w[k, 0:128, :] = hi
        w[k, 128:256, :] = lo

    def plane(d):
        return (z + 8 - d) % 8

    def piece(d, e):
        return g.at[plane(d) * 2 + (xh if e == 0 else 1 - xh), rows(c, pos)]

    def both(d):
        return g.at[pl.ds(plane(d) * 2, 2), rows(c, pos)]

    def recv_first(d):
        for e in ((1,) if d == 0 else (0, 1)):
            pltpu.make_async_remote_copy(
                src_ref=piece(d, e), dst_ref=piece(d, e), send_sem=s1.at[e, d], recv_sem=r1.at[e, d],
                device_id=twin, device_id_type=MESH).wait_recv()

    def relay(ref, d, e, device, start):
        cp = pltpu.make_async_remote_copy(
            src_ref=ref, dst_ref=ref, send_sem=s1.at[e, d], recv_sem=r1.at[e, d],
            device_id=device, device_id_type=MESH)
        if start:
            cp.start()
            later.append(cp)
        else:
            cp.wait_recv()

    def relayed(d):
        if d == 4:
            relay(piece(4, 0), 4, 0, near[2], False)
            relay(piece(4, 1), 4, 1, near[6], False)
        else:
            relay(both(d), d, 0, near[1 if d == 3 else 7], False)

    later = []
    for i, d in enumerate(ORDER):
        weights(2 * i)
        weights(2 * i + 1)
        if d == 0:
            mine.wait()
        if d in (3, 4, 5):
            relayed(d)
        else:
            recv_first(d)
        if d == 2:
            relay(both(2), 3, 0, near[1], True)
            relay(piece(2, 0), 4, 0, near[2], True)
        if d == 6:
            relay(both(6), 5, 0, near[7], True)
            relay(piece(6, 1), 4, 1, near[6], True)
        zz = plane(d)
        part = g.at[pl.ds(zz * 2, 2), rows(c, pos)]
        for j in (2, 1, 3):
            cp = pltpu.make_async_remote_copy(
                src_ref=part, dst_ref=part, send_sem=s2.at[j, d], recv_sem=r2.at[j, d],
                device_id=ring[j], device_id_type=MESH)
            cp.start()
            later.append(cp)
        cp = pltpu.make_async_remote_copy(
            src_ref=part, dst_ref=part, send_sem=s3.at[0, d], recv_sem=r3.at[0, d],
            device_id=twin, device_id_type=MESH)
        cp.start()
        later.append(cp)

    for d in ORDER:
        zz = (z + 8 - d) % 8
        for j in (1, 3, 2):
            part = g.at[pl.ds(zz * 2, 2), rows(c, (pos + 4 - j) % 4)]
            pltpu.make_async_remote_copy(
                src_ref=part, dst_ref=part, send_sem=s2.at[j, d], recv_sem=r2.at[j, d],
                device_id=ring[j], device_id_type=MESH).wait_recv()
            cp = pltpu.make_async_remote_copy(
                src_ref=part, dst_ref=part, send_sem=s3.at[j, d], recv_sem=r3.at[j, d],
                device_id=twin, device_id_type=MESH)
            cp.start()
            later.append(cp)
    other_pos = c * x + (1 - c) * y
    for d in ORDER:
        zz = (z + 8 - d) % 8
        for j in range(4):
            part = g.at[pl.ds(zz * 2, 2), rows(1 - c, (other_pos + 4 - j) % 4)]
            pltpu.make_async_remote_copy(
                src_ref=part, dst_ref=part, send_sem=s3.at[j, d], recv_sem=r3.at[j, d],
                device_id=twin, device_id_type=MESH).wait_recv()
    for cp in first + later:
        cp.wait_send()


def gather(row, cd, airr, own, amp, integ):
    smem = pl.BlockSpec(memory_space=pltpu.SMEM)
    vmem = pl.BlockSpec(memory_space=pltpu.VMEM)
    hbm = pl.BlockSpec(memory_space=pl.ANY)
    dma = pltpu.SemaphoreType.DMA
    return pl.pallas_call(
        gather_kernel,
        out_shape=(
            jax.ShapeDtypeStruct((16, SLOTS * 8, 128), F32),
            jax.ShapeDtypeStruct((KT, 256, 128), BF16),
            jax.ShapeDtypeStruct((8, 128), jnp.int32),
            jax.ShapeDtypeStruct((1,), jnp.int32),
        ),
        in_specs=[smem, smem, smem, vmem, vmem, hbm, hbm],
        out_specs=(vmem, vmem, vmem, smem),
        scratch_shapes=[
            pltpu.VMEM((SLOTS * 8, 128), F32),
            pltpu.VMEM((1, 128), jnp.int32),
            pltpu.SMEM((1, 128), jnp.int32),
            pltpu.VMEM((IRREPS * VB // 8, 8, KT * CD_TILE), F32),
            pltpu.VMEM((OWN_TILES * KT, ROW_TILE, CD_TILE), F32),
            dma, dma, dma, dma, dma((2, 8)), dma((2, 8)), dma((4, 8)), dma((4, 8)), dma((4, 8)), dma((4, 8)),
        ],
        compiler_params=pltpu.CompilerParams(
            collective_id=0, has_side_effects=True, vmem_limit_bytes=24 * 2**20),
        name="gather",
    )(row, cd, airr, row.reshape(1, TILES), own, amp, integ)


def product_kernel(tab, g, w, p, lhs, acc):
    p[ZEROT] = jnp.zeros((8, 128), F32)

    def label(lab, c):
        first = tab[T_START, lab]
        nr = tab[T_START, lab + 1] - first
        nk = tab[T_NK, lab]

        def rowsof(m, c):
            tiles = []
            for t in range(MT):
                ok = m * MT + t < nr
                v = tab[T_LST, first + jnp.minimum(m * MT + t, nr - 1)]
                tiles.append((jnp.where(ok, v & 255, DUMPT), v >> 8))
            acc[...] = jnp.zeros_like(acc)

            def depth(kc, c):
                ks = [kc * KC + h for h in range(KC)]
                have = [k < nk for k in ks]
                cols = [tab[T_KL, lab * KT + jnp.where(ok, k, 0)] for ok, k in zip(have, ks)]
                for t in range(MT):
                    off = tiles[t][1]
                    for h in range(KC):
                        src = g[jnp.minimum(off + jnp.where(have[h], ks[h], 0), 16 * SLOTS - 1)]
                        if h > 0:
                            src = jnp.where(have[h], src, 0.0)
                        lhs[t * 8:(t + 1) * 8, h * 128:(h + 1) * 128] = src
                a = lhs[...]
                hi = a.astype(BF16)
                lo = (a - hi.astype(F32)).astype(BF16)
                ww = jnp.concatenate([w[k] for k in cols], axis=1)
                nt = (((1,), (1,)), ((), ()))
                big = lax.dot_general(hi, ww, nt, preferred_element_type=F32)
                small = lax.dot_general(lo, ww[:128], nt, preferred_element_type=F32)
                acc[...] += big[:, :128] + (big[:, 128:] + small)
                return c

            lax.fori_loop(0, (nk + KC - 1) // KC, depth, 0)
            for t in range(MT):
                p[tiles[t][0]] = acc[t * 8:(t + 1) * 8, :]
            return c

        return lax.fori_loop(0, (nr + MT - 1) // MT, rowsof, c)

    lax.fori_loop(0, IRREPS, label, 0)


def product(tab, g, w):
    smem = pl.BlockSpec(memory_space=pltpu.SMEM)
    vmem = pl.BlockSpec(memory_space=pltpu.VMEM)
    return pl.pallas_call(
        product_kernel,
        out_shape=jax.ShapeDtypeStruct((PT, 8, 128), F32),
        in_specs=[smem, vmem, vmem],
        out_specs=vmem,
        scratch_shapes=[pltpu.VMEM((MT * 8, KC * 128), F32), pltpu.VMEM((MT * 8, 128), F32)],
        compiler_params=pltpu.CompilerParams(vmem_limit_bytes=24 * 2**20),
        name="product",
    )(tab, g, w)


def owners_kernel(tab, p, out, send, loc_sem, ss, rs):
    me = lax.axis_index("slab")
    barrier = pltpu.get_barrier_semaphore()
    for i in range(1, 16):
        pl.semaphore_signal(barrier, inc=1, device_id={"slab": (me + i) % 16}, device_id_type=MESH)
    copies = []
    for i in list(range(1, 16)) + [0]:
        o = (me + i) % 16
        block = jnp.concatenate([p[tab[T_SRC + o // 8, o % 8 * CAP + q]] for q in range(CAP)], axis=0)
        send[i] = jnp.transpose(block)[:VP]
        if i == 1:
            pl.semaphore_wait(barrier, 15)
        if i == 0:
            cp = pltpu.make_async_copy(send.at[i], out.at[me], loc_sem)
        else:
            cp = pltpu.make_async_remote_copy(
                src_ref=send.at[i], dst_ref=out.at[me], send_sem=ss.at[i], recv_sem=rs.at[i],
                device_id={"slab": o}, device_id_type=MESH)
        cp.start()
        copies.append(cp)
    for i in range(1, 16):
        src = (me + 16 - i) % 16
        pltpu.make_async_remote_copy(
            src_ref=send.at[i], dst_ref=out.at[src], send_sem=ss.at[i], recv_sem=rs.at[i],
            device_id={"slab": (me + i) % 16}, device_id_type=MESH).wait_recv()
    for cp in copies[:-1]:
        cp.wait_send()
    copies[-1].wait()


def owners(tab, p):
    smem = pl.BlockSpec(memory_space=pltpu.SMEM)
    vmem = pl.BlockSpec(memory_space=pltpu.VMEM)
    dma = pltpu.SemaphoreType.DMA
    return pl.pallas_call(
        owners_kernel,
        out_shape=jax.ShapeDtypeStruct((16, VP, 128), F32),
        in_specs=[smem, vmem],
        out_specs=vmem,
        scratch_shapes=[pltpu.VMEM((16, VP, 128), F32), dma, dma((16,)), dma((16,))],
        compiler_params=pltpu.CompilerParams(
            collective_id=1, has_side_effects=True, vmem_limit_bytes=24 * 2**20),
        name="owners",
    )(tab, p)


def expand_kernel(airr, tab, arrived, out, stage, sems):
    blk = lax.axis_index("blk")
    lab = tab[T_LAB:T_LAB + 1, :]
    upper = lax.broadcasted_iota(jnp.int32, (8, 128), 0) < 4

    def one(s, c):
        want = lab ^ airr[s, blk]
        block = arrived[s]
        moved = jnp.concatenate([block[100:104], block[0:100]], axis=0)
        for m in range(IRREPS // 2):
            even = want == 2 * m
            odd = want == 2 * m + 1
            base = 2 * VB * m
            stage[s, base:base + 96, :] = jnp.where(even, block[:96], 0.0)
            stage[s, base + 96:base + 104, :] = jnp.where(
                upper, jnp.where(even, block[96:], 0.0), jnp.where(odd, moved[:8], 0.0))
            stage[s, base + 104:base + 200, :] = jnp.where(odd, moved[8:], 0.0)
        pltpu.make_async_copy(stage.at[s], out.at[s], sems.at[s]).start()
        return c

    lax.fori_loop(0, 16, one, 0)
    for s in range(16):
        pltpu.make_async_copy(stage.at[s], out.at[s], sems.at[s]).wait()


def expand(airr, tab, arrived):
    return pl.pallas_call(
        expand_kernel,
        out_shape=jax.ShapeDtypeStruct((16, IRREPS * VB, 128), F32),
        in_specs=[pl.BlockSpec(memory_space=pltpu.SMEM)] + [pl.BlockSpec(memory_space=pltpu.VMEM)] * 2,
        out_specs=pl.BlockSpec(memory_space=pl.ANY),
        scratch_shapes=[pltpu.VMEM((16, IRREPS * VB, 128), F32), pltpu.SemaphoreType.DMA((16,))],
        compiler_params=pltpu.CompilerParams(vmem_limit_bytes=40 * 2**20),
        name="expand",
    )(airr, tab, arrived)


def dense(amplitude, integ, row, cd, airr, tab):
    slab = lax.axis_index("slab")
    blk = lax.axis_index("blk")
    own_a = airr[slab, blk]
    copies = jnp.broadcast_to(amplitude[None], (16,) + amplitude.shape)
    piece = lax.all_to_all(copies, "blk", split_axis=0, concat_axis=0, tiled=True).reshape(-1, KT * CD_TILE)
    cd_cols = jnp.repeat(cd, CD_TILE)
    labels = jnp.repeat(row, ROW_TILE)
    coupled = jnp.where(labels[:, None] == cd_cols[None, :], piece, 0.0)
    blocks = integ.reshape(IRREPS, VB, KT * CD_TILE)
    want = cd_cols ^ own_a
    kept = jnp.sum(jnp.where(want[None, None, :] == jnp.arange(IRREPS)[:, None, None], blocks, 0.0), axis=0)
    prod = jnp.dot(coupled, kept.T, precision=lax.Precision.HIGHEST, preferred_element_type=F32)
    prod = jnp.concatenate([prod.reshape(TILES, ROW_TILE, VB), jnp.zeros((1, ROW_TILE, VB), F32)], axis=0)
    packed = jnp.take(prod, tab[T_SRC:T_SRC + 2].reshape(-1), axis=0).reshape(16, CAP * ROW_TILE, VB)
    arrived = lax.all_to_all(packed, "slab", split_axis=0, concat_axis=0, tiled=True)
    arrived = jnp.transpose(arrived, (0, 2, 1))
    return jnp.pad(arrived, ((0, 0), (0, VP - VB), (0, 0)))


def shards(amplitude, integrals, row, cd, airr, owner):
    integ = integrals.reshape(KT * CD_TILE, IRREPS * VB).T
    amp = amplitude.reshape(OWN_TILES, ROW_TILE, KT, CD_TILE).transpose(0, 2, 1, 3)
    g, w, tab, fit = gather(
        row, cd, airr, owner.reshape(1, TILES), amp.reshape(OWN_TILES * KT, ROW_TILE, CD_TILE),
        integ.reshape(IRREPS * VB // 8, 8, KT * CD_TILE))

    p = product(tab, g.reshape(16 * SLOTS, 8, 128), w)

    def fast(amplitude, integ, row, cd, airr, tab, p):
        return owners(tab, p)

    def slow(amplitude, integ, row, cd, airr, tab, p):
        return dense(amplitude, integ, row, cd, airr, tab)

    arrived = lax.cond(fit[0] == 1, fast, slow, amplitude, integ, row, cd, airr, tab, p)
    out = expand(airr, tab, arrived)
    return jnp.transpose(out, (2, 0, 1)).reshape(CAP * ROW_TILE, 16, 1, IRREPS * VB)


def solution(mesh):
    return jax.shard_map(
        shards,
        mesh=mesh,
        in_specs=(P("blk", None), P(None, "slab", "blk", None), P(), P(), P(), P()),
        out_specs=P("slab", None, "blk", None),
        check_vma=False,
    )
```

time: 56.6 us -> 52.1 us (0.920)
  Pallas kernels: 54 us -> 50 us
    pallas_call x1 -> x0, Pallas kernels: 3.58 us -> none  [prep(): pl.pallas_call(prep_kernel, out_shape=(jax.ShapeDtypeStruct(((SLOTS + 1)...]
    pallas_call x1, Pallas kernels: 16 us -> 15.4 us  [owners(): pl.pallas_call(owners_kernel, out_shape=jax.ShapeDtypeStruct((16, VP, 128...]
    slice x1 -> x0, local copies, waits for them, and re-layouts: 0.58 us -> none  [shards(): tab[T_FIT] == 1]
where the time goes in v3:
time: 52.1 us; the launch traced here: 51.5 us
  Pallas kernels  50 us (96%)
  between operations  0.74 us (1%)
  local copies, waits for them, and re-layouts  0.69 us (1%)
    pallas_call x1, Pallas kernels, gather(): pl.pallas_call(gather_kernel, out_shape=(jax.ShapeDtypeStruct((16, SLOTS...  26.6 us
    pallas_call x1, Pallas kernels, owners(): pl.pallas_call(owners_kernel, out_shape=jax.ShapeDtypeStruct((16, VP, 128...  15.4 us
    pallas_call x1, Pallas kernels, product(): pl.pallas_call(product_kernel, out_shape=jax.ShapeDtypeStruct((PT, 8, 128...  4.36 us
    pallas_call x1, Pallas kernels, expand(): pl.pallas_call(expand_kernel, out_shape=jax.ShapeDtypeStruct((16, IRREPS...  3.58 us

profile of v3, /device:TPU:1, one launch (start us, length us, event | category | flops | bytes accessed | tf_op | source)
XLA Modules:
  0.0 51.5 jit_solution(6347831330180840112)
XLA Ops:
  0.0 0.0 copy-start.3
  0.0 0.0 copy-start.4
  0.0 0.0 copy-start
  0.0 0.7 %copy-done = s32[128,1]{0,1:T(1,128)S(1)} copy-done((s32[128,1]{0,1:T(1,128)S(1)}, s32[128,1]{0,1:T(1,128)}, u32[]{:S(2)}) %copy-start) | copy-done | bytes 536
  0.7 0.0 copy-start.1
  0.7 0.0 copy-start.2
  0.7 26.6 %gather.9 = (f32[16,256,128]{2,1,0:T(8,128)S(1)}, bf16[16,256,128]{2,1,0:T(8,128)(2,1)S(1)}, s32[8,128]{1,0:T(8,128)S(1)}, s32[1]{0:T(128)}) custom-call(s32[128]{0:T(128)} %row.1, s32[16]{0:T(128)} %cd.1, s32[16,16]{1,0:T(8,128)} %airr.3, s32[1,128]{1,0:T(1,128)} %bitcast.43, s32[1,128]{1,0:T(1,128)S(1)} %bitcast.36, f32[128,8,128]{2,1,0:T(8,128)} %bitcast.41, ...), custom_call_target="tpu_custom_call" | custom-call | tf_op jit(solution)/shard_map/gather/pallas_call | solution.py:263
  28.0 4.4 %product.1 = f32[136,8,128]{2,1,0:T(8,128)S(1)} custom-call(s32[8,128]{1,0:T(8,128)S(1)} %get-tuple-element.36.tab, f32[512,8,128]{2,1,0:T(8,128)S(1)} %bitcast.35, bf16[16,256,128]{2,1,0:T(8,128)(2,1)S(1)} %get-tuple-element.39.w), custom_call_target="tpu_custom_call" | custom-call | tf_op jit(solution)/shard_map/product/pallas_call | solution.py:337
  32.4 0.0 copy-done.3
  32.4 0.0 copy-done.4
  32.4 0.0 copy-done.1
  32.4 0.0 copy-done.2
  32.4 15.5 %conditional.1 = (f32[16,104,128]{2,1,0:T(8,128)S(1)}) conditional(s32[]{:T(128)} %bitcast.17, (s32[8,128]{1,0:T(8,128)S(1)}, s32[128]{0:T(128)S(1)}, s32[16]{0:T(128)S(1)}, f32[64,2048]{1,0:T(8,128)S(1)}, s32[16,16]{1,0:T(8,128)S(1)}, /*index=5*/f32[800,2048]{1,0:T(8,128)}) %tuple.19, (s32[8,128]{1,0:T(8,128)S(1)}, ...), branch_computations={%region_0.2_spmd, %region_2.3_spmd} | conditional | flops 2524075264 | bytes 73312184 | solution.py:466
  32.5 15.4 %owners.1 = f32[16,104,128]{2,1,0:T(8,128)S(1)} custom-call(s32[8,128]{1,0:T(8,128)S(1)} %get-tuple-element.30.tab, f32[136,8,128]{2,1,0:T(8,128)S(1)} %get-tuple-element.31.p), custom_call_target="tpu_custom_call" | custom-call | tf_op jit(solution)/shard_map/cond/branch_1_fun/owners/pallas_call | solution.py:382
  47.9 3.6 %expand.1 = f32[16,800,128]{2,1,0:T(8,128)} custom-call(s32[16,16]{1,0:T(8,128)S(1)} %copy-done.2, s32[8,128]{1,0:T(8,128)S(1)} %get-tuple-element.36.tab, f32[16,104,128]{2,1,0:T(8,128)S(1)} %get-tuple-element.40.arrived), custom_call_target="tpu_custom_call" | custom-call | tf_op jit(solution)/shard_map/expand/pallas_call | solution.py:420
Async XLA Ops:
  0.0 32.4 %copy-start.3 = (s32[128]{0:T(128)S(1)}, s32[128]{0:T(128)}, u32[]{:S(2)}) copy-start(s32[128]{0:T(128)} %row.1) | copy-start | bytes 1540
  0.0 32.4 %copy-start.4 = (s32[16]{0:T(128)S(1)}, s32[16]{0:T(128)}, u32[]{:S(2)}) copy-start(s32[16]{0:T(128)} %cd.1) | copy-start | bytes 196
  0.0 0.7 %copy-start = (s32[128,1]{0,1:T(1,128)S(1)}, s32[128,1]{0,1:T(1,128)}, u32[]{:S(2)}) copy-start(s32[128,1]{0,1:T(1,128)} %param.13) | copy-start | bytes 1540
  0.7 31.7 %copy-start.1 = (f32[64,2048]{1,0:T(8,128)S(1)}, f32[64,2048]{1,0:T(8,128)}, u32[]{:S(2)}) copy-start(f32[64,2048]{1,0:T(8,128)} %param.8) | copy-start | bytes 1572868
  0.7 31.7 %copy-start.2 = (s32[16,16]{1,0:T(8,128)S(1)}, s32[16,16]{1,0:T(8,128)}, u32[]{:S(2)}) copy-start(s32[16,16]{1,0:T(8,128)} %airr.3) | copy-start | bytes 3076

commit v4 on v3

--- a/solution.py
+++ b/solution.py
@@ -20,6 +20,7 @@
 ZEROT = 128
 DUMPT = 129
 PT = 136
+SENT = 100
 MT = 24
 KC = 2
 T_LST = 0
@@ -116,45 +117,46 @@
         cp.start()
         first.append(cp)
 
-    row_l = row_v[...]
-    own_l = own_v[...]
-    diag = sub == lane
-    row_c = jnp.sum(jnp.where(diag, row_l, 0), axis=1, keepdims=True)
-    own_c = jnp.sum(jnp.where(diag, own_l, 0), axis=1, keepdims=True)
-    before = lane < sub
-    sub_c = lax.broadcasted_iota(jnp.int32, (128, 1), 0)
-    rank = jnp.sum(jnp.where((own_l == own_c) & before, 1, 0), axis=1, keepdims=True)
-    target = own_c * CAP + rank
-    for h in range(2):
-        tab[T_SRC + h:T_SRC + h + 1, :] = ZEROT + jnp.sum(
-            jnp.where(target == lane + h * 128, sub - ZEROT, 0), axis=0, keepdims=True)
-    tab[T_LAB:T_LAB + 1, :] = jnp.sum(
-        jnp.where(target == slab * CAP + lane // ROW_TILE, row_c, 0), axis=0, keepdims=True)
-    order = jnp.sum(jnp.where((row_l < row_c) | ((row_l == row_c) & before), 1, 0), axis=1, keepdims=True)
-    nk_l = jnp.zeros((1, 128), jnp.int32)
-    nk_c = jnp.zeros((128, 1), jnp.int32)
-    nk_of = jnp.zeros((1, 128), jnp.int32)
-    list_l = jnp.zeros((1, 128), jnp.int32)
-    for k in range(KT):
-        nk_l = nk_l + jnp.where(row_l == labs[k], 1, 0)
-        nk_c = nk_c + jnp.where(row_c == labs[k], 1, 0)
-        nk_of = nk_of + jnp.where(one_lane == labs[k], 1, 0)
-        kap = jnp.int32(0)
-        for other in range(k):
-            kap = kap + jnp.where(labs[other] == labs[k], 1, 0)
-        list_l = list_l + jnp.where(one_lane == labs[k] * KT + kap, k, 0)
-    same = (lane // OWN_TILES == sub // OWN_TILES) & before
-    inside = jnp.sum(jnp.where(same, nk_l, 0), axis=1, keepdims=True)
-    value = sub_c + 256 * (SLOTS * (sub_c // OWN_TILES) + inside)
-    tab[T_LST:T_LST + 1, :] = jnp.sum(jnp.where(order == lane, value, 0), axis=0, keepdims=True)
-    tab[T_START:T_START + 1, :] = jnp.sum(jnp.where(row_c < lane, 1, 0), axis=0, keepdims=True)
-    tab[T_KL:T_KL + 1, :] = list_l
-    tab[T_NK:T_NK + 1, :] = nk_of
-    tab[7:8, :] = jnp.zeros((1, 128), jnp.int32)
-    fit[0] = jnp.where(jnp.max(inside + nk_c) <= SLOTS, 1, 0)
-
     raw_copy.wait()
     own_a = airr[slab, blk]
+
+    def tables():
+        row_l = row_v[...]
+        own_l = own_v[...]
+        diag = sub == lane
+        row_c = jnp.sum(jnp.where(diag, row_l, 0), axis=1, keepdims=True)
+        own_c = jnp.sum(jnp.where(diag, own_l, 0), axis=1, keepdims=True)
+        before = lane < sub
+        sub_c = lax.broadcasted_iota(jnp.int32, (128, 1), 0)
+        rank = jnp.sum(jnp.where((own_l == own_c) & before, 1, 0), axis=1, keepdims=True)
+        target = own_c * CAP + rank
+        for h in range(2):
+            tab[T_SRC + h:T_SRC + h + 1, :] = ZEROT + jnp.sum(
+                jnp.where(target == lane + h * 128, sub - ZEROT, 0), axis=0, keepdims=True)
+        tab[T_LAB:T_LAB + 1, :] = jnp.sum(
+            jnp.where(target == slab * CAP + lane // ROW_TILE, row_c, 0), axis=0, keepdims=True)
+        order = jnp.sum(jnp.where((row_l < row_c) | ((row_l == row_c) & before), 1, 0), axis=1, keepdims=True)
+        nk_l = jnp.zeros((1, 128), jnp.int32)
+        nk_c = jnp.zeros((128, 1), jnp.int32)
+        nk_of = jnp.zeros((1, 128), jnp.int32)
+        list_l = jnp.zeros((1, 128), jnp.int32)
+        for k in range(KT):
+            nk_l = nk_l + jnp.where(row_l == labs[k], 1, 0)
+            nk_c = nk_c + jnp.where(row_c == labs[k], 1, 0)
+            nk_of = nk_of + jnp.where(one_lane == labs[k], 1, 0)
+            kap = jnp.int32(0)
+            for other in range(k):
+                kap = kap + jnp.where(labs[other] == labs[k], 1, 0)
+            list_l = list_l + jnp.where(one_lane == labs[k] * KT + kap, k, 0)
+        same = (lane // OWN_TILES == sub // OWN_TILES) & before
+        inside = jnp.sum(jnp.where(same, nk_l, 0), axis=1, keepdims=True)
+        value = sub_c + 256 * (SLOTS * (sub_c // OWN_TILES) + inside)
+        tab[T_LST:T_LST + 1, :] = jnp.sum(jnp.where(order == lane, value, 0), axis=0, keepdims=True)
+        tab[T_START:T_START + 1, :] = jnp.sum(jnp.where(row_c < lane, 1, 0), axis=0, keepdims=True)
+        tab[T_KL:T_KL + 1, :] = list_l
+        tab[T_NK:T_NK + 1, :] = nk_of
+        tab[7:8, :] = jnp.zeros((1, 128), jnp.int32)
+        fit[0] = jnp.where(jnp.max(inside + nk_c) <= SLOTS, 1, 0)
 
     def weights(k):
         beta = labs[k] ^ own_a
@@ -164,10 +166,11 @@
         moved = jnp.concatenate([block[4:], block[:4]], axis=0)
         block = jnp.where(odd == 1, moved, block)
         block = jnp.concatenate([block, jnp.zeros((128 - VP, 128), F32)], axis=0)
+        block = jnp.transpose(block)
         hi = block.astype(BF16)
         lo = (block - hi.astype(F32)).astype(BF16)
-        w[k, 0:128, :] = hi
-        w[k, 128:256, :] = lo
+        w[k, :, 0:128] = hi
+        w[k, :, 128:256] = lo
 
     def plane(d):
         return (z + 8 - d) % 8
@@ -203,8 +206,13 @@
 
     later = []
     for i, d in enumerate(ORDER):
-        weights(2 * i)
-        weights(2 * i + 1)
+        if d == 0:
+            for k in range(8):
+                weights(k)
+        if d == 3:
+            tables()
+            for k in range(8, KT):
+                weights(k)
         if d == 0:
             mine.wait()
         if d in (3, 4, 5):
@@ -225,11 +233,12 @@
                 device_id=ring[j], device_id_type=MESH)
             cp.start()
             later.append(cp)
-        cp = pltpu.make_async_remote_copy(
-            src_ref=part, dst_ref=part, send_sem=s3.at[0, d], recv_sem=r3.at[0, d],
+
+    def half(d, c_):
+        ref = g.at[pl.ds((z + 8 - d) % 8 * 2, 2), pl.ds(pl.multiple_of(c_ * 128, 128), 128)]
+        return pltpu.make_async_remote_copy(
+            src_ref=ref, dst_ref=ref, send_sem=s3.at[d], recv_sem=r3.at[d],
             device_id=twin, device_id_type=MESH)
-        cp.start()
-        later.append(cp)
 
     for d in ORDER:
         zz = (z + 8 - d) % 8
@@ -238,19 +247,10 @@
             pltpu.make_async_remote_copy(
                 src_ref=part, dst_ref=part, send_sem=s2.at[j, d], recv_sem=r2.at[j, d],
                 device_id=ring[j], device_id_type=MESH).wait_recv()
-            cp = pltpu.make_async_remote_copy(
-                src_ref=part, dst_ref=part, send_sem=s3.at[j, d], recv_sem=r3.at[j, d],
-                device_id=twin, device_id_type=MESH)
-            cp.start()
-            later.append(cp)
-    other_pos = c * x + (1 - c) * y
+        later.append(half(d, c))
+        later[-1].start()
     for d in ORDER:
-        zz = (z + 8 - d) % 8
-        for j in range(4):
-            part = g.at[pl.ds(zz * 2, 2), rows(1 - c, (other_pos + 4 - j) % 4)]
-            pltpu.make_async_remote_copy(
-                src_ref=part, dst_ref=part, send_sem=s3.at[j, d], recv_sem=r3.at[j, d],
-                device_id=twin, device_id_type=MESH).wait_recv()
+        half(d, 1 - c).wait_recv()
     for cp in first + later:
         cp.wait_send()
 
@@ -264,7 +264,7 @@
         gather_kernel,
         out_shape=(
             jax.ShapeDtypeStruct((16, SLOTS * 8, 128), F32),
-            jax.ShapeDtypeStruct((KT, 256, 128), BF16),
+            jax.ShapeDtypeStruct((KT, 128, 256), BF16),
             jax.ShapeDtypeStruct((8, 128), jnp.int32),
             jax.ShapeDtypeStruct((1,), jnp.int32),
         ),
@@ -276,7 +276,7 @@
             pltpu.SMEM((1, 128), jnp.int32),
             pltpu.VMEM((IRREPS * VB // 8, 8, KT * CD_TILE), F32),
             pltpu.VMEM((OWN_TILES * KT, ROW_TILE, CD_TILE), F32),
-            dma, dma, dma, dma, dma((2, 8)), dma((2, 8)), dma((4, 8)), dma((4, 8)), dma((4, 8)), dma((4, 8)),
+            dma, dma, dma, dma, dma((2, 8)), dma((2, 8)), dma((4, 8)), dma((4, 8)), dma((8,)), dma((8,)),
         ],
         compiler_params=pltpu.CompilerParams(
             collective_id=0, has_side_effects=True, vmem_limit_bytes=24 * 2**20),
@@ -314,10 +314,9 @@
                 a = lhs[...]
                 hi = a.astype(BF16)
                 lo = (a - hi.astype(F32)).astype(BF16)
-                ww = jnp.concatenate([w[k] for k in cols], axis=1)
-                nt = (((1,), (1,)), ((), ()))
-                big = lax.dot_general(hi, ww, nt, preferred_element_type=F32)
-                small = lax.dot_general(lo, ww[:128], nt, preferred_element_type=F32)
+                ww = jnp.concatenate([w[k] for k in cols], axis=0)
+                big = jnp.dot(hi, ww, preferred_element_type=F32)
+                small = jnp.dot(lo, ww[:, :128], preferred_element_type=F32)
                 acc[...] += big[:, :128] + (big[:, 128:] + small)
                 return c
 
@@ -347,32 +346,45 @@
 
 def owners_kernel(tab, p, out, send, loc_sem, ss, rs):
     me = lax.axis_index("slab")
+    c = me % 2
+    y = (me // 2) % 4
+    xl = me // 8
+    steps = [(a, b, e) for a, b in ((1, 2), (0, 2), (1, 1), (1, 3), (0, 1), (0, 3), (1, 0)) for e in (0, 1)] + [(0, 0, 1)]
+    targets = [(xl + a) % 2 * 8 + (y + b) % 4 * 2 + (c + e) % 2 for a, b, e in steps]
+    sources = [(xl + a) % 2 * 8 + (y + 4 - b) % 4 * 2 + (c + e) % 2 for a, b, e in steps]
     barrier = pltpu.get_barrier_semaphore()
-    for i in range(1, 16):
-        pl.semaphore_signal(barrier, inc=1, device_id={"slab": (me + i) % 16}, device_id_type=MESH)
+    for o in targets:
+        pl.semaphore_signal(barrier, inc=1, device_id={"slab": o}, device_id_type=MESH)
+
+    def make(i, o):
+        block = jnp.concatenate([p[tab[T_SRC + o // 8, o % 8 * CAP + q]] for q in range(CAP)], axis=0)
+        send[i] = jnp.transpose(block)[:SENT]
+
+    def copy(i, o, place):
+        return pltpu.make_async_remote_copy(
+            src_ref=send.at[i], dst_ref=out.at[place], send_sem=ss.at[i], recv_sem=rs.at[i],
+            device_id={"slab": o}, device_id_type=MESH)
+
+    EARLY = 4
     copies = []
-    for i in list(range(1, 16)) + [0]:
-        o = (me + i) % 16
-        block = jnp.concatenate([p[tab[T_SRC + o // 8, o % 8 * CAP + q]] for q in range(CAP)], axis=0)
-        send[i] = jnp.transpose(block)[:VP]
-        if i == 1:
+    for i, o in enumerate(targets):
+        make(i, o)
+        if i == EARLY - 1:
             pl.semaphore_wait(barrier, 15)
-        if i == 0:
-            cp = pltpu.make_async_copy(send.at[i], out.at[me], loc_sem)
-        else:
-            cp = pltpu.make_async_remote_copy(
-                src_ref=send.at[i], dst_ref=out.at[me], send_sem=ss.at[i], recv_sem=rs.at[i],
-                device_id={"slab": o}, device_id_type=MESH)
-        cp.start()
-        copies.append(cp)
-    for i in range(1, 16):
-        src = (me + 16 - i) % 16
-        pltpu.make_async_remote_copy(
-            src_ref=send.at[i], dst_ref=out.at[src], send_sem=ss.at[i], recv_sem=rs.at[i],
-            device_id={"slab": (me + i) % 16}, device_id_type=MESH).wait_recv()
-    for cp in copies[:-1]:
+            for j in range(EARLY):
+                copies.append(copy(j, targets[j], me))
+                copies[-1].start()
+        elif i >= EARLY:
+            copies.append(copy(i, o, me))
+            copies[-1].start()
+    make(15, me)
+    local = pltpu.make_async_copy(send.at[15], out.at[me], loc_sem)
+    local.start()
+    for i, o in enumerate(sources):
+        copy(i, o, o).wait_recv()
+    for cp in copies:
         cp.wait_send()
-    copies[-1].wait()
+    local.wait()
 
 
 def owners(tab, p):
@@ -381,10 +393,10 @@
     dma = pltpu.SemaphoreType.DMA
     return pl.pallas_call(
         owners_kernel,
-        out_shape=jax.ShapeDtypeStruct((16, VP, 128), F32),
+        out_shape=jax.ShapeDtypeStruct((16, SENT, 128), F32),
         in_specs=[smem, vmem],
         out_specs=vmem,
-        scratch_shapes=[pltpu.VMEM((16, VP, 128), F32), dma, dma((16,)), dma((16,))],
+        scratch_shapes=[pltpu.VMEM((16, SENT, 128), F32), dma, dma((16,)), dma((16,))],
         compiler_params=pltpu.CompilerParams(
             collective_id=1, has_side_effects=True, vmem_limit_bytes=24 * 2**20),
         name="owners",
@@ -399,6 +411,7 @@
     def one(s, c):
         want = lab ^ airr[s, blk]
         block = arrived[s]
+        block = jnp.concatenate([block, block[0:4]], axis=0)
         moved = jnp.concatenate([block[100:104], block[0:100]], axis=0)
         for m in range(IRREPS // 2):
             even = want == 2 * m
@@ -445,7 +458,7 @@
     packed = jnp.take(prod, tab[T_SRC:T_SRC + 2].reshape(-1), axis=0).reshape(16, CAP * ROW_TILE, VB)
     arrived = lax.all_to_all(packed, "slab", split_axis=0, concat_axis=0, tiled=True)
     arrived = jnp.transpose(arrived, (0, 2, 1))
-    return jnp.pad(arrived, ((0, 0), (0, VP - VB), (0, 0)))
+    return arrived
 
 
 def shards(amplitude, integrals, row, cd, airr, owner):

time: 52.1 us -> 50.4 us (0.967)
  Pallas kernels: 50 us -> 48.8 us
where the time goes in v4:
time: 50.4 us; the launch traced here: 50.3 us
  Pallas kernels  48.8 us (97%)
  between operations  0.74 us (1%)
  local copies, waits for them, and re-layouts  0.69 us (1%)
    pallas_call x1, Pallas kernels, gather(): pl.pallas_call(gather_kernel, out_shape=(jax.ShapeDtypeStruct((16, SLOTS...  26.2 us
    pallas_call x1, Pallas kernels, owners(): pl.pallas_call(owners_kernel, out_shape=jax.ShapeDtypeStruct((16, SENT, 1...  15.1 us
    pallas_call x1, Pallas kernels, product(): pl.pallas_call(product_kernel, out_shape=jax.ShapeDtypeStruct((PT, 8, 128...  3.87 us
    pallas_call x1, Pallas kernels, expand(): pl.pallas_call(expand_kernel, out_shape=jax.ShapeDtypeStruct((16, IRREPS...  3.58 us

profile of v4, /device:TPU:1, one launch (start us, length us, event | category | flops | bytes accessed | tf_op | source)
XLA Modules:
  0.0 50.3 jit_solution(14074638339992935279)
XLA Ops:
  0.0 0.0 copy-start.3
  0.0 0.0 copy-start.4
  0.0 0.0 copy-start
  0.0 0.7 %copy-done = s32[128,1]{0,1:T(1,128)S(1)} copy-done((s32[128,1]{0,1:T(1,128)S(1)}, s32[128,1]{0,1:T(1,128)}, u32[]{:S(2)}) %copy-start) | copy-done | bytes 536
  0.7 0.0 copy-start.1
  0.7 0.0 copy-start.2
  0.7 26.2 %gather.9 = (f32[16,256,128]{2,1,0:T(8,128)S(1)}, bf16[16,128,256]{2,1,0:T(8,128)(2,1)S(1)}, s32[8,128]{1,0:T(8,128)S(1)}, s32[1]{0:T(128)}) custom-call(s32[128]{0:T(128)} %row.1, s32[16]{0:T(128)} %cd.1, s32[16,16]{1,0:T(8,128)} %airr.3, s32[1,128]{1,0:T(1,128)} %bitcast.43, s32[1,128]{1,0:T(1,128)S(1)} %bitcast.36, f32[128,8,128]{2,1,0:T(8,128)} %bitcast.41, ...), custom_call_target="tpu_custom_call" | custom-call | tf_op jit(solution)/shard_map/gather/pallas_call | solution.py:263
  27.6 3.9 %product.1 = f32[136,8,128]{2,1,0:T(8,128)S(1)} custom-call(s32[8,128]{1,0:T(8,128)S(1)} %get-tuple-element.36.tab, f32[512,8,128]{2,1,0:T(8,128)S(1)} %bitcast.35, bf16[16,128,256]{2,1,0:T(8,128)(2,1)S(1)} %get-tuple-element.39.w), custom_call_target="tpu_custom_call" | custom-call | tf_op jit(solution)/shard_map/product/pallas_call | solution.py:336
  31.5 0.0 copy-done.3
  31.5 0.0 copy-done.4
  31.5 0.0 copy-done.1
  31.5 0.0 copy-done.2
  31.5 15.2 %conditional.1 = (f32[16,100,128]{2,1,0:T(8,128)S(1)}) conditional(s32[]{:T(128)} %bitcast.17, (s32[8,128]{1,0:T(8,128)S(1)}, s32[128]{0:T(128)S(1)}, s32[16]{0:T(128)S(1)}, f32[64,2048]{1,0:T(8,128)S(1)}, s32[16,16]{1,0:T(8,128)S(1)}, /*index=5*/f32[800,2048]{1,0:T(8,128)}) %tuple.19, (s32[8,128]{1,0:T(8,128)S(1)}, ...), branch_computations={%region_0.2_spmd, %region_2.3_spmd} | conditional | flops 2524075264 | bytes 71641008 | solution.py:479
  31.5 15.1 %owners.1 = f32[16,100,128]{2,1,0:T(8,128)S(1)} custom-call(s32[8,128]{1,0:T(8,128)S(1)} %get-tuple-element.30.tab, f32[136,8,128]{2,1,0:T(8,128)S(1)} %get-tuple-element.31.p), custom_call_target="tpu_custom_call" | custom-call | tf_op jit(solution)/shard_map/cond/branch_1_fun/owners/pallas_call | solution.py:394
  46.7 3.6 %expand.1 = f32[16,800,128]{2,1,0:T(8,128)} custom-call(s32[16,16]{1,0:T(8,128)S(1)} %copy-done.2, s32[8,128]{1,0:T(8,128)S(1)} %get-tuple-element.36.tab, f32[16,100,128]{2,1,0:T(8,128)S(1)} %get-tuple-element.40.arrived), custom_call_target="tpu_custom_call" | custom-call | tf_op jit(solution)/shard_map/expand/pallas_call | solution.py:433
Async XLA Ops:
  0.0 31.5 %copy-start.3 = (s32[128]{0:T(128)S(1)}, s32[128]{0:T(128)}, u32[]{:S(2)}) copy-start(s32[128]{0:T(128)} %row.1) | copy-start | bytes 1540
  0.0 31.5 %copy-start.4 = (s32[16]{0:T(128)S(1)}, s32[16]{0:T(128)}, u32[]{:S(2)}) copy-start(s32[16]{0:T(128)} %cd.1) | copy-start | bytes 196
  0.0 0.7 %copy-start = (s32[128,1]{0,1:T(1,128)S(1)}, s32[128,1]{0,1:T(1,128)}, u32[]{:S(2)}) copy-start(s32[128,1]{0,1:T(1,128)} %param.13) | copy-start | bytes 1540
  0.7 30.8 %copy-start.1 = (f32[64,2048]{1,0:T(8,128)S(1)}, f32[64,2048]{1,0:T(8,128)}, u32[]{:S(2)}) copy-start(f32[64,2048]{1,0:T(8,128)} %param.8) | copy-start | bytes 1572868
  0.7 30.8 %copy-start.2 = (s32[16,16]{1,0:T(8,128)S(1)}, s32[16,16]{1,0:T(8,128)}, u32[]{:S(2)}) copy-start(s32[16,16]{1,0:T(8,128)} %airr.3) | copy-start | bytes 3076

commit v5 on v4

--- a/solution.py
+++ b/solution.py
@@ -23,6 +23,7 @@
 SENT = 100
 MT = 24
 KC = 2
+GATHERED = 20
 T_LST = 0
 T_SRC = 1
 T_START = 3
@@ -263,7 +264,7 @@
     return pl.pallas_call(
         gather_kernel,
         out_shape=(
-            jax.ShapeDtypeStruct((16, SLOTS * 8, 128), F32),
+            jax.ShapeDtypeStruct((GATHERED, SLOTS * 8, 128), F32),
             jax.ShapeDtypeStruct((KT, 128, 256), BF16),
             jax.ShapeDtypeStruct((8, 128), jnp.int32),
             jax.ShapeDtypeStruct((1,), jnp.int32),
@@ -284,7 +285,7 @@
     )(row, cd, airr, row.reshape(1, TILES), own, amp, integ)
 
 
-def product_kernel(tab, g, w, p, lhs, acc):
+def product_kernel(tab, g, w, p, acc):
     p[ZEROT] = jnp.zeros((8, 128), F32)
 
     def label(lab, c):
@@ -304,14 +305,12 @@
                 ks = [kc * KC + h for h in range(KC)]
                 have = [k < nk for k in ks]
                 cols = [tab[T_KL, lab * KT + jnp.where(ok, k, 0)] for ok, k in zip(have, ks)]
-                for t in range(MT):
-                    off = tiles[t][1]
-                    for h in range(KC):
-                        src = g[jnp.minimum(off + jnp.where(have[h], ks[h], 0), 16 * SLOTS - 1)]
-                        if h > 0:
-                            src = jnp.where(have[h], src, 0.0)
-                        lhs[t * 8:(t + 1) * 8, h * 128:(h + 1) * 128] = src
-                a = lhs[...]
+                at = [jnp.where(ok, k, 0) for ok, k in zip(have, ks)]
+                parts = []
+                for h in range(KC):
+                    part = jnp.concatenate([g[tiles[t][1] + at[h]] for t in range(MT)], axis=0)
+                    parts.append(part if h == 0 else jnp.where(have[h], part, 0.0))
+                a = jnp.concatenate(parts, axis=1)
                 hi = a.astype(BF16)
                 lo = (a - hi.astype(F32)).astype(BF16)
                 ww = jnp.concatenate([w[k] for k in cols], axis=0)
@@ -338,7 +337,7 @@
         out_shape=jax.ShapeDtypeStruct((PT, 8, 128), F32),
         in_specs=[smem, vmem, vmem],
         out_specs=vmem,
-        scratch_shapes=[pltpu.VMEM((MT * 8, KC * 128), F32), pltpu.VMEM((MT * 8, 128), F32)],
+        scratch_shapes=[pltpu.VMEM((MT * 8, 128), F32)],
         compiler_params=pltpu.CompilerParams(vmem_limit_bytes=24 * 2**20),
         name="product",
     )(tab, g, w)
@@ -441,7 +440,7 @@
     )(airr, tab, arrived)
 
 
-def dense(amplitude, integ, row, cd, airr, tab):
+def dense(amplitude, integ, row, cd, airr, owner):
     slab = lax.axis_index("slab")
     blk = lax.axis_index("blk")
     own_a = airr[slab, blk]
@@ -455,7 +454,13 @@
     kept = jnp.sum(jnp.where(want[None, None, :] == jnp.arange(IRREPS)[:, None, None], blocks, 0.0), axis=0)
     prod = jnp.dot(coupled, kept.T, precision=lax.Precision.HIGHEST, preferred_element_type=F32)
     prod = jnp.concatenate([prod.reshape(TILES, ROW_TILE, VB), jnp.zeros((1, ROW_TILE, VB), F32)], axis=0)
-    packed = jnp.take(prod, tab[T_SRC:T_SRC + 2].reshape(-1), axis=0).reshape(16, CAP * ROW_TILE, VB)
+    own = owner[:, 0]
+    tiles = jnp.arange(TILES, dtype=jnp.int32)
+    ahead = (own[:, None] == own[None, :]) & (tiles[None, :] < tiles[:, None])
+    target = own * CAP + jnp.sum(ahead.astype(jnp.int32), axis=1)
+    hit = target[None, :] == jnp.arange(16 * CAP, dtype=jnp.int32)[:, None]
+    source = ZEROT + jnp.sum(jnp.where(hit, tiles[None, :] - ZEROT, 0), axis=1)
+    packed = jnp.take(prod, source, axis=0).reshape(16, CAP * ROW_TILE, VB)
     arrived = lax.all_to_all(packed, "slab", split_axis=0, concat_axis=0, tiled=True)
     arrived = jnp.transpose(arrived, (0, 2, 1))
     return arrived
@@ -468,15 +473,15 @@
         row, cd, airr, owner.reshape(1, TILES), amp.reshape(OWN_TILES * KT, ROW_TILE, CD_TILE),
         integ.reshape(IRREPS * VB // 8, 8, KT * CD_TILE))
 
-    p = product(tab, g.reshape(16 * SLOTS, 8, 128), w)
-
-    def fast(amplitude, integ, row, cd, airr, tab, p):
+    p = product(tab, g.reshape(GATHERED * SLOTS, 8, 128), w)
+
+    def fast(amplitude, integ, row, cd, airr, owner, tab, p):
         return owners(tab, p)
 
-    def slow(amplitude, integ, row, cd, airr, tab, p):
-        return dense(amplitude, integ, row, cd, airr, tab)
-
-    arrived = lax.cond(fit[0] == 1, fast, slow, amplitude, integ, row, cd, airr, tab, p)
+    def slow(amplitude, integ, row, cd, airr, owner, tab, p):
+        return dense(amplitude, integ, row, cd, airr, owner)
+
+    arrived = lax.cond(fit[0] == 1, fast, slow, amplitude, integ, row, cd, airr, owner, tab, p)
     out = expand(airr, tab, arrived)
     return jnp.transpose(out, (2, 0, 1)).reshape(CAP * ROW_TILE, 16, 1, IRREPS * VB)
 

time: 50.4 us -> 49.5 us (0.982)
  local copies, waits for them, and re-layouts: 0.69 us -> 0.02 us
    unnamed x10, local copies, waits for them, and re-layouts: 0.69 us -> 0.02 us
where the time goes in v5:
time: 49.5 us; the launch traced here: 49.4 us
  Pallas kernels  48.7 us (98%)
  between operations  0.69 us (1%)
    pallas_call x1, Pallas kernels, gather(): pl.pallas_call(gather_kernel, out_shape=(jax.ShapeDtypeStruct((GATHERED,...  26.4 us
    pallas_call x1, Pallas kernels, owners(): pl.pallas_call(owners_kernel, out_shape=jax.ShapeDtypeStruct((16, SENT, 1...  15.1 us
    pallas_call x1, Pallas kernels, product(): pl.pallas_call(product_kernel, out_shape=jax.ShapeDtypeStruct((PT, 8, 128...  3.59 us
    pallas_call x1, Pallas kernels, expand(): pl.pallas_call(expand_kernel, out_shape=jax.ShapeDtypeStruct((16, IRREPS...  3.58 us

profile of v5, /device:TPU:1, one launch (start us, length us, event | category | flops | bytes accessed | tf_op | source)
XLA Modules:
  0.0 49.4 jit_solution(16387901624486078771)
XLA Ops:
  0.0 0.0 copy-start.1
  0.0 0.0 copy-start.2
  0.0 0.0 copy-start.3
  0.0 0.0 copy-start.4
  0.0 0.0 copy-start
  0.0 26.4 %gather.9 = (f32[20,256,128]{2,1,0:T(8,128)S(1)}, bf16[16,128,256]{2,1,0:T(8,128)(2,1)S(1)}, s32[8,128]{1,0:T(8,128)S(1)}, s32[1]{0:T(128)}) custom-call(s32[128]{0:T(128)} %row.1, s32[16]{0:T(128)} %cd.1, s32[16,16]{1,0:T(8,128)} %airr.3, s32[1,128]{1,0:T(1,128)} %bitcast.46, s32[1,128]{1,0:T(1,128)} %bitcast.48, f32[128,8,128]{2,1,0:T(8,128)} %bitcast.43, ...), custom_call_target="tpu_custom_call" | custom-call | tf_op jit(solution)/shard_map/gather/pallas_call | solution.py:264
  27.0 3.6 %product.1 = f32[136,8,128]{2,1,0:T(8,128)S(1)} custom-call(s32[8,128]{1,0:T(8,128)S(1)} %get-tuple-element.36.tab, f32[640,8,128]{2,1,0:T(8,128)S(1)} %bitcast.38, bf16[16,128,256]{2,1,0:T(8,128)(2,1)S(1)} %get-tuple-element.39.w), custom_call_target="tpu_custom_call" | custom-call | tf_op jit(solution)/shard_map/product/pallas_call | solution.py:335
  30.6 0.0 copy-done.1
  30.6 0.0 copy-done.2
  30.6 0.0 copy-done.3
  30.6 0.0 copy-done.4
  30.6 0.0 copy-done
  30.6 15.2 %conditional.1 = (f32[16,100,128]{2,1,0:T(8,128)S(1)}) conditional(s32[]{:T(128)} %bitcast.19, (s32[128,1]{0,1:T(1,128)S(1)}, s32[128]{0:T(128)S(1)}, s32[16]{0:T(128)S(1)}, f32[64,2048]{1,0:T(8,128)S(1)}, s32[16,16]{1,0:T(8,128)S(1)}, /*index=5*/f32[800,2048]{1,0:T(8,128)}) %tuple.21, (s32[8,128]{1,0:T(8,128)S(1)}, ...), branch_computations={%region_0.4_spmd, %region_4.5_spmd} | conditional | flops 2524255488 | bytes 71651248 | solution.py:484
  30.7 15.1 %owners.1 = f32[16,100,128]{2,1,0:T(8,128)S(1)} custom-call(s32[8,128]{1,0:T(8,128)S(1)} %get-tuple-element.30.tab, f32[136,8,128]{2,1,0:T(8,128)S(1)} %get-tuple-element.31.p), custom_call_target="tpu_custom_call" | custom-call | tf_op jit(solution)/shard_map/cond/branch_1_fun/owners/pallas_call | solution.py:393
  45.8 3.6 %expand.1 = f32[16,800,128]{2,1,0:T(8,128)} custom-call(s32[16,16]{1,0:T(8,128)S(1)} %copy-done.1, s32[8,128]{1,0:T(8,128)S(1)} %get-tuple-element.36.tab, f32[16,100,128]{2,1,0:T(8,128)S(1)} %get-tuple-element.42.arrived), custom_call_target="tpu_custom_call" | custom-call | tf_op jit(solution)/shard_map/expand/pallas_call | solution.py:432
Async XLA Ops:
  0.0 30.6 %copy-start.1 = (s32[16,16]{1,0:T(8,128)S(1)}, s32[16,16]{1,0:T(8,128)}, u32[]{:S(2)}) copy-start(s32[16,16]{1,0:T(8,128)} %airr.3) | copy-start | bytes 3076
  0.0 30.6 %copy-start.2 = (s32[128]{0:T(128)S(1)}, s32[128]{0:T(128)}, u32[]{:S(2)}) copy-start(s32[128]{0:T(128)} %row.1) | copy-start | bytes 1540
  0.0 30.6 %copy-start.3 = (s32[16]{0:T(128)S(1)}, s32[16]{0:T(128)}, u32[]{:S(2)}) copy-start(s32[16]{0:T(128)} %cd.1) | copy-start | bytes 196
  0.0 30.6 %copy-start.4 = (s32[128,1]{0,1:T(1,128)S(1)}, s32[128,1]{0,1:T(1,128)}, u32[]{:S(2)}) copy-start(s32[128,1]{0,1:T(1,128)} %param.13) | copy-start | bytes 1540
  0.0 30.6 %copy-start = (f32[64,2048]{1,0:T(8,128)S(1)}, f32[64,2048]{1,0:T(8,128)}, u32[]{:S(2)}) copy-start(f32[64,2048]{1,0:T(8,128)} %param.8) | copy-start | bytes 1572868

commit v6 on v5

--- a/solution.py
+++ b/solution.py
@@ -423,7 +423,7 @@
         pltpu.make_async_copy(stage.at[s], out.at[s], sems.at[s]).start()
         return c
 
-    lax.fori_loop(0, 16, one, 0)
+    lax.fori_loop(0, 16, one, 0, unroll=4)
     for s in range(16):
         pltpu.make_async_copy(stage.at[s], out.at[s], sems.at[s]).wait()
 

time: 49.5 us -> 49.8 us (level)
  no operation moved by 1% of the time
where the time goes in v6:
time: 49.8 us; the launch traced here: 49.6 us
  Pallas kernels  48.9 us (98%)
  between operations  0.69 us (1%)
    pallas_call x1, Pallas kernels, gather(): pl.pallas_call(gather_kernel, out_shape=(jax.ShapeDtypeStruct((GATHERED,...  26.4 us
    pallas_call x1, Pallas kernels, owners(): pl.pallas_call(owners_kernel, out_shape=jax.ShapeDtypeStruct((16, SENT, 1...  15.1 us
    pallas_call x1, Pallas kernels, product(): pl.pallas_call(product_kernel, out_shape=jax.ShapeDtypeStruct((PT, 8, 128...  3.81 us
    pallas_call x1, Pallas kernels, expand(): pl.pallas_call(expand_kernel, out_shape=jax.ShapeDtypeStruct((16, IRREPS...  3.58 us

profile of v6, /device:TPU:1, one launch (start us, length us, event | category | flops | bytes accessed | tf_op | source)
XLA Modules:
  0.0 49.6 jit_solution(15304151270843328627)
XLA Ops:
  0.0 0.0 copy-start.1
  0.0 0.0 copy-start.2
  0.0 0.0 copy-start.3
  0.0 0.0 copy-start.4
  0.0 0.0 copy-start
  0.0 26.4 %gather.9 = (f32[20,256,128]{2,1,0:T(8,128)S(1)}, bf16[16,128,256]{2,1,0:T(8,128)(2,1)S(1)}, s32[8,128]{1,0:T(8,128)S(1)}, s32[1]{0:T(128)}) custom-call(s32[128]{0:T(128)} %row.1, s32[16]{0:T(128)} %cd.1, s32[16,16]{1,0:T(8,128)} %airr.3, s32[1,128]{1,0:T(1,128)} %bitcast.46, s32[1,128]{1,0:T(1,128)} %bitcast.48, f32[128,8,128]{2,1,0:T(8,128)} %bitcast.43, ...), custom_call_target="tpu_custom_call" | custom-call | tf_op jit(solution)/shard_map/gather/pallas_call | solution.py:264
  27.0 3.8 %product.1 = f32[136,8,128]{2,1,0:T(8,128)S(1)} custom-call(s32[8,128]{1,0:T(8,128)S(1)} %get-tuple-element.36.tab, f32[640,8,128]{2,1,0:T(8,128)S(1)} %bitcast.38, bf16[16,128,256]{2,1,0:T(8,128)(2,1)S(1)} %get-tuple-element.39.w), custom_call_target="tpu_custom_call" | custom-call | tf_op jit(solution)/shard_map/product/pallas_call | solution.py:335
  30.8 0.0 copy-done.1
  30.8 0.0 copy-done.2
  30.8 0.0 copy-done.3
  30.9 0.0 copy-done.4
  30.9 0.0 copy-done
  30.9 15.2 %conditional.1 = (f32[16,100,128]{2,1,0:T(8,128)S(1)}) conditional(s32[]{:T(128)} %bitcast.19, (s32[128,1]{0,1:T(1,128)S(1)}, s32[128]{0:T(128)S(1)}, s32[16]{0:T(128)S(1)}, f32[64,2048]{1,0:T(8,128)S(1)}, s32[16,16]{1,0:T(8,128)S(1)}, /*index=5*/f32[800,2048]{1,0:T(8,128)}) %tuple.21, (s32[8,128]{1,0:T(8,128)S(1)}, ...), branch_computations={%region_0.4_spmd, %region_4.5_spmd} | conditional | flops 2524255488 | bytes 71651248 | solution.py:484
  30.9 15.1 %owners.1 = f32[16,100,128]{2,1,0:T(8,128)S(1)} custom-call(s32[8,128]{1,0:T(8,128)S(1)} %get-tuple-element.30.tab, f32[136,8,128]{2,1,0:T(8,128)S(1)} %get-tuple-element.31.p), custom_call_target="tpu_custom_call" | custom-call | tf_op jit(solution)/shard_map/cond/branch_1_fun/owners/pallas_call | solution.py:393
  46.0 3.6 %expand.1 = f32[16,800,128]{2,1,0:T(8,128)} custom-call(s32[16,16]{1,0:T(8,128)S(1)} %copy-done.1, s32[8,128]{1,0:T(8,128)S(1)} %get-tuple-element.36.tab, f32[16,100,128]{2,1,0:T(8,128)S(1)} %get-tuple-element.42.arrived), custom_call_target="tpu_custom_call" | custom-call | tf_op jit(solution)/shard_map/expand/pallas_call | solution.py:432
Async XLA Ops:
  0.0 30.8 %copy-start.1 = (s32[16,16]{1,0:T(8,128)S(1)}, s32[16,16]{1,0:T(8,128)}, u32[]{:S(2)}) copy-start(s32[16,16]{1,0:T(8,128)} %airr.3) | copy-start | bytes 3076
  0.0 30.8 %copy-start.2 = (s32[128]{0:T(128)S(1)}, s32[128]{0:T(128)}, u32[]{:S(2)}) copy-start(s32[128]{0:T(128)} %row.1) | copy-start | bytes 1540
  0.0 30.8 %copy-start.3 = (s32[16]{0:T(128)S(1)}, s32[16]{0:T(128)}, u32[]{:S(2)}) copy-start(s32[16]{0:T(128)} %cd.1) | copy-start | bytes 196
  0.0 30.8 %copy-start.4 = (s32[128,1]{0,1:T(1,128)S(1)}, s32[128,1]{0,1:T(1,128)}, u32[]{:S(2)}) copy-start(s32[128,1]{0,1:T(1,128)} %param.13) | copy-start | bytes 1540
  0.0 30.8 %copy-start = (f32[64,2048]{1,0:T(8,128)S(1)}, f32[64,2048]{1,0:T(8,128)}, u32[]{:S(2)}) copy-start(f32[64,2048]{1,0:T(8,128)} %param.8) | copy-start | bytes 1572868
